TPU v7x, 32 devices: a whole 2x2x4 slice. The times are simulated.
32 devices in a mesh: gx: 8 (over y, x, core), gy: 4 (over z).
Axes of the slice: x: 2, y: 2, z: 4, core: 2. Of those that a mesh axis runs over, the one named last changes fastest.
Arguments:
- field_in: bfloat16 [32, 16, 1024], P('gx', 'gy'), may hold values from -6 to 6
- w_first: bfloat16 [27, 64, 64], replicated, may hold values from -0.15625 to 0.15625
- b_first: float32 [64], replicated, may hold values from -3 to 3
- w_upper: bfloat16 [8, 64, 64], replicated, may hold values from -0.75 to 0.75
- w_second: bfloat16 [27, 64, 64], replicated, may hold values from -0.15625 to 0.15625
- b_second: float32 [64], replicated, may hold values from -3 to 3
- cotangent: bfloat16 [64, 32, 2048], P('gx', 'gy'), may hold values from -6 to 6
- tile_weights: int32 [8, 4], P('gx', 'gy'), may hold values from 0 to 3
Outputs:
- output_field: bfloat16 [64, 32, 2048], P('gx', 'gy')
- grad_input: bfloat16 [32, 16, 1024], P('gx', 'gy')
- grad_first: float32 [27, 64, 64], replicated
- grad_upper: float32 [8, 64, 64], replicated
- grad_second: float32 [27, 64, 64], replicated
All inputs are finite; a program needn't handle non-finite values.
Results may differ from a plain program's by a relative error of at most 0.01.
Values may be sent and summed in bfloat16 or wider, within the bound.
A program may use at most 64 MiB of HBM per device.

v0:
```python
import math

import jax
import jax.numpy as jnp
from jax import lax
from jax.sharding import PartitionSpec as P


def extended(cells, sides, width):
    for axis, dim in sides:
        count = lax.axis_size(axis)
        head = lax.slice_in_dim(cells, 0, width, axis=dim)
        tail = lax.slice_in_dim(cells, cells.shape[dim] - width, cells.shape[dim], axis=dim)
        cells = jnp.concatenate(
            [
                lax.ppermute(tail, axis, [(i, (i + 1) % count) for i in range(count)]),
                cells,
                lax.ppermute(head, axis, [((i + 1) % count, i) for i in range(count)]),
            ],
            axis=dim,
        )
    return cells


def act(v):
    return 0.2 * v + 0.8 * jax.nn.softplus(v)


def slope(v):
    return 0.2 + 0.8 * jax.nn.sigmoid(v)


def depth_pad(field):
    return jnp.pad(field, ((0, 0), (0, 0), (1, 1), (0, 0)))


def conv_local(padded, weights, rows, cols):
    depth = padded.shape[2] - 2
    chans = padded.shape[3]
    total = jnp.zeros((rows * cols * depth, weights.shape[2]), jnp.float32)
    for k in range(27):
        ox, oy, oz = (k // 9, k // 3 % 3, k % 3)
        piece = padded[ox : ox + rows, oy : oy + cols, oz : oz + depth].reshape(-1, chans)
        total = total + jnp.dot(piece, weights[k], preferred_element_type=jnp.float32)
    return total.reshape(rows, cols, depth, -1)


def wgrad_local(padded, grad):
    rows, cols, depth, chans = grad.shape
    flat_grad = grad.reshape(-1, chans)
    terms = []
    for k in range(27):
        ox, oy, oz = (k // 9, k // 3 % 3, k % 3)
        piece = padded[ox : ox + rows, oy : oy + cols, oz : oz + depth].reshape(-1, padded.shape[3])
        terms.append(
            lax.dot_general(
                piece, flat_grad, (((0,), (0,)), ((), ())), preferred_element_type=jnp.float32
            )
        )
    return jnp.stack(terms)


def flip_taps(weights):
    return jnp.transpose(weights[::-1], (0, 2, 1))


def upsample(hidden, upper_taps):
    rows, cols, depth, chans = hidden.shape
    fine = jnp.einsum("xyze,abced->xaybzcd", hidden, upper_taps, preferred_element_type=jnp.float32)
    return fine.reshape(2 * rows, 2 * cols, 2 * depth, chans).astype(jnp.bfloat16)


def per_device(field_in, w_first, b_first, w_upper, w_second, b_second, cotangent, tile_weights):
    rows, cols, flat = field_in.shape
    chans = w_first.shape[1]
    depth = flat // chans
    upper_taps = w_upper.reshape(2, 2, 2, chans, chans)
    taps_wide = w_upper.astype(jnp.float32).reshape(2, 2, 2, chans, chans)
    rim = extended(field_in, (("gx", 0), ("gy", 1)), 1)
    input_pad = depth_pad(rim.reshape(rows + 2, cols + 2, depth, chans))
    pre_first = conv_local(input_pad, w_first, rows, cols) + b_first
    hidden = act(pre_first).astype(jnp.bfloat16)
    upper = upsample(hidden, upper_taps)
    upper_cycle = extended(upper.reshape(2 * rows, 2 * cols, 2 * flat), (("gx", 0), ("gy", 1)), 1)
    upper_pad = depth_pad(upper_cycle.reshape(2 * rows + 2, 2 * cols + 2, 2 * depth, chans))
    pre_second = conv_local(upper_pad, w_second, 2 * rows, 2 * cols) + b_second
    output_field = act(pre_second).astype(jnp.bfloat16)
    tiles_x, tiles_y = tile_weights.shape
    side = 2 * rows // tiles_x
    weight_grid = tile_weights.astype(jnp.float32)[:, None, :, None, None, None]
    fine_cot = cotangent.reshape(tiles_x, side, tiles_y, side, 2 * depth, chans).astype(jnp.float32)
    slope_fine = slope(pre_second).reshape(tiles_x, side, tiles_y, side, 2 * depth, chans)
    grad_pre = (
        (weight_grid * fine_cot * slope_fine)
        .reshape(2 * rows, 2 * cols, 2 * depth, chans)
        .astype(jnp.bfloat16)
    )
    devices = lax.axis_size("gx") * lax.axis_size("gy")
    coarse_scale = 1.0 / math.sqrt(rows * cols * depth * devices)
    fine_scale = 1.0 / math.sqrt(8 * rows * cols * depth * devices)
    grad_cycle = extended(grad_pre.reshape(2 * rows, 2 * cols, 2 * flat), (("gx", 0), ("gy", 1)), 1)
    grad_pad = depth_pad(grad_cycle.reshape(2 * rows + 2, 2 * cols + 2, 2 * depth, chans))
    grad_upper_field = conv_local(grad_pad, flip_taps(w_second), 2 * rows, 2 * cols)
    grad_six = grad_upper_field.reshape(rows, 2, cols, 2, depth, 2, chans)
    grad_hidden = jnp.einsum("xaybzcd,abced->xyze", grad_six, taps_wide)
    upper_term = jnp.einsum("xyze,xaybzcd->abced", hidden.astype(jnp.float32), grad_six)
    upper_term = upper_term.reshape(8, chans, chans) * coarse_scale
    grad_pre_first = (grad_hidden * slope(pre_first)).astype(jnp.bfloat16)
    coarse_cycle = extended(grad_pre_first.reshape(rows, cols, flat), (("gx", 0), ("gy", 1)), 1)
    coarse_pad = depth_pad(coarse_cycle.reshape(rows + 2, cols + 2, depth, chans))
    grad_input = conv_local(coarse_pad, flip_taps(w_first), rows, cols).astype(jnp.bfloat16)
    second_term = wgrad_local(upper_pad, grad_pre)
    first_term = wgrad_local(input_pad, grad_pre_first) * coarse_scale
    grad_first, grad_upper, grad_second = lax.psum(
        (first_term, upper_term, second_term * fine_scale), ("gx", "gy")
    )
    return (
        output_field.reshape(2 * rows, 2 * cols, 2 * flat),
        grad_input.reshape(rows, cols, flat),
        grad_first,
        grad_upper,
        grad_second,
    )


def solution(mesh):
    in_specs = (P("gx", "gy", None), P(), P(), P(), P(), P(), P("gx", "gy", None), P("gx", "gy"))
    out_specs = (P("gx", "gy", None), P("gx", "gy", None), P(), P(), P())
    return jax.shard_map(
        per_device, mesh=mesh, in_specs=in_specs, out_specs=out_specs, check_vma=False
    )
```

profile of v0, /device:TPU:0, one launch (start us, length us, event | category | flops | bytes accessed | tf_op | source)
XLA Modules:
  0.0 257.4 jit_solution(4771590456210279036)
XLA Ops:
  7.2 0.8 fusion.189
  8.0 0.5 collective-permute-start
  8.5 2.9 %collective-permute-start.1 = (bf16[1,4,1024]{2,1,0:T(4,128)(2,1)S(1)}, bf16[1,4,1024]{2,1,0:T(4,128)(2,1)S(1)}, u32[]{:S(2)}, u32[]{:S(2)}) collective-permute-start(bf16[1,4,1024]{2,1,0:T(4,128)(2,1)S(1)} %get-tuple-element.133), channel_id=1, source_target_pairs={{4,0},{8,4},{12,8},{16,12},{20,16},{24,20},{28,24},{0,28},{5,1},{9... | collective-permute-start | bytes 24584 | tf_op jit(solution)/shard_map/ppermute | solution.py:18
  11.4 1.3 collective-permute-done
  12.7 0.8 constant_dynamic-update-slice_fusion.1
  13.6 2.4 collective-permute-start.2
  15.9 2.1 collective-permute-start.3
  18.0 1.8 collective-permute-done.2
  20.7 0.6 copy-done.4
  27.2 0.5 copy.21
  28.0 0.8 reverse_bitcast_fusion
  29.4 2.7 %collective-permute-start.5 = (bf16[1,8,2048]{2,1,0:T(8,128)(2,1)S(1)}, bf16[1,8,2048]{2,1,0:T(8,128)(2,1)S(1)}, u32[]{:S(2)}, u32[]{:S(2)}) collective-permute-start(bf16[1,8,2048]{2,1,0:T(8,128)(2,1)S(1)} %slice.865), channel_id=1, source_target_pairs={{4,0},{8,4},{12,8},{16,12},{20,16},{24,20},{28,24},{0,28},{5,1},{9... | collective-permute-start | bytes 98312 | tf_op jit(solution)/shard_map/ppermute | solution.py:18
  32.2 1.4 collective-permute-done.5
  33.8 1.4 collective-permute-start.6
  35.1 2.5 collective-permute-start.7
  37.6 0.8 reverse_bitcast_fusion.1
  39.2 0.8 copy.27
  39.9 0.5 collective-permute-done.6
  40.5 0.6 collective-permute-done.7
  41.4 0.8 reshape.491
  42.2 4.1 %pad_slice_fusion.18 = (bf16[8,8,32,64]{3,2,1,0:T(8,128)(2,1)S(1)}, bf16[8,8,32,64]{3,2,1,0:T(8,128)(2,1)S(1)}, bf16[8,8,32,64]{3,2,1,0:T(8,128)(2,1)S(1)}, bf16...) fusion(bf16[10,10,32,64]{3,2,1,0:T(8,128)(2,1)S(1)} %reshape.491), kind=kLoop, calls=%fused_computation.242 | loop fusion | bytes 6848512 | tf_op jit(solution)/shard_map/slice | solution.py:43
  46.3 0.9 fusion.180
  57.0 2.2 multiply_convert_fusion.1
  59.2 1.4 mul.89
  60.6 1.6 multiply_convert_fusion
  67.7 0.5 fusion.29
  71.1 2.7 %collective-permute-start.9 = (bf16[1,8,2048]{2,1,0:T(8,128)(2,1)S(1)}, bf16[1,8,2048]{2,1,0:T(8,128)(2,1)S(1)}, u32[]{:S(2)}, u32[]{:S(2)}) collective-permute-start(bf16[1,8,2048]{2,1,0:T(8,128)(2,1)S(1)} %slice.925), channel_id=1, source_target_pairs={{4,0},{8,4},{12,8},{16,12},{20,16},{24,20},{28,24},{0,28},{5,1},{9... | collective-permute-start | bytes 98312 | tf_op jit(solution)/shard_map/ppermute | solution.py:18
  74.1 1.1 collective-permute-done.8
  75.5 1.3 collective-permute-start.10
  76.8 2.6 collective-permute-start.11
  79.4 1.0 broadcast_multiply_fusion
  80.4 2.2 collective-permute-done.10
  82.9 0.8 reshape.521
  83.8 3.9 %pad_slice_fusion = (bf16[8,8,32,64]{3,2,1,0:T(8,128)(2,1)S(1)}, bf16[8,8,32,64]{3,2,1,0:T(8,128)(2,1)S(1)}, bf16[8,8,32,64]{3,2,1,0:T(8,128)(2,1)S(1)}, bf16[8,...) fusion(bf16[10,10,32,64]{3,2,1,0:T(8,128)(2,1)S(1)} %reshape.521), kind=kLoop, calls=%fused_computation.224 | loop fusion | bytes 6848512 | tf_op jit(solution)/shard_map/slice | solution.py:43
  87.7 0.9 fusion.179
  103.1 1.0 broadcast_multiply_fusion.1
  104.4 2.6 %collective-permute-start.13 = (bf16[1,4,1024]{2,1,0:T(4,128)(2,1)S(1)}, bf16[1,4,1024]{2,1,0:T(4,128)(2,1)S(1)}, u32[]{:S(2)}, u32[]{:S(2)}) collective-permute-start(bf16[1,4,1024]{2,1,0:T(4,128)(2,1)S(1)} %slice.985), channel_id=1, source_target_pairs={{4,0},{8,4},{12,8},{16,12},{20,16},{24,20},{28,24},{0,28},{5,1},{9... | collective-permute-start | bytes 24584 | tf_op jit(solution)/shard_map/ppermute | solution.py:18
  107.1 1.2 collective-permute-done.13
  108.4 0.8 collective-permute-start.14
  109.2 3.0 %collective-permute-start.15 = (bf16[6,1,1024]{2,1,0:T(2,128)(2,1)S(1)}, bf16[6,1,1024]{2,1,0:T(2,128)(2,1)S(1)}, u32[]{:S(2)}, u32[]{:S(2)}) collective-permute-start(bf16[6,1,1024]{2,1,0:T(2,128)(2,1)S(1)} %get-tuple-element.130), channel_id=1, source_target_pairs={{1,0},{2,1},{3,2},{0,3},{5,4},{6,5},{7,6},{4,7},{9,8},{10,9},{11,1... | collective-permute-start | bytes 36872 | tf_op jit(solution)/shard_map/ppermute | solution.py:18
  112.6 0.8 copy.30
  113.5 0.7 collective-permute-done.14
  114.8 0.6 copy-done.3
  119.8 0.7 convert_element_type.73
  120.5 126.1 %all-reduce.7.cloned.1.call-done = (f32[27,64,64]{2,1,0:T(8,128)}, f32[8,64,64]{2,1,0:T(8,128)}, f32[27,64,64]{2,1,0:T(8,128)}) async-done(((f32[27,64,64]{2,1,0:T(8,128)}, f32[8,64,64]{2,1,0:T(8,128)}, f32[27,64,64]{2,1,0:T(8,128)}), (f32[27,64,64]{2,1,0:T(8,128)}, f32[8,64,64]{2,1,0:T(8,128)}, f32[27,64,64]{2,1,0:T(8,128)})) %all-reduce.7.cloned.1.call-update) | async-done | bytes 1015824 | tf_op jit(solution)/shard_map/psum | solution.py:114
  246.6 2.3 copy.156
  248.9 0.7 copy.157
  249.6 0.9 copy.158
  (234 shorter events, 46.9 us)
Async XLA Ops:
  7.2 19.8 %copy-start = (bf16[8,64,64]{2,1,0:T(8,128)(2,1)S(1)}, bf16[8,64,64]{2,1,0:T(8,128)(2,1)}, u32[]{:S(2)}) copy-start(bf16[8,64,64]{2,1,0:T(8,128)(2,1)} %param.11) | copy-start | bytes 196612
  7.2 239.5 %all-reduce.7.cloned.1.call-start = ((), (), s32[]{:S(2)}) async-start(), calls=%async_computation | async-start | bytes 4063232 | tf_op jit(solution)/shard_map/psum | solution.py:114
  8.0 4.7 %collective-permute-start = (bf16[1,4,1024]{2,1,0:T(4,128)(2,1)S(1)}, bf16[1,4,1024]{2,1,0:T(4,128)(2,1)S(1)}, u32[]{:S(2)}, u32[]{:S(2)}) collective-permute-start(bf16[1,4,1024]{2,1,0:T(4,128)(2,1)S(1)} %get-tuple-element.134), channel_id=1, source_target_pairs={{0,4},{4,8},{8,12},{12,16},{16,20},{20,24},{24,28},{28,0},{1,5},{5... | collective-permute-start | bytes 24584 | tf_op jit(solution)/shard_map/ppermute | solution.py:16
  8.5 5.0 %collective-permute-start.1 = (bf16[1,4,1024]{2,1,0:T(4,128)(2,1)S(1)}, bf16[1,4,1024]{2,1,0:T(4,128)(2,1)S(1)}, u32[]{:S(2)}, u32[]{:S(2)}) collective-permute-start(bf16[1,4,1024]{2,1,0:T(4,128)(2,1)S(1)} %get-tuple-element.133), channel_id=1, source_target_pairs={{4,0},{8,4},{12,8},{16,12},{20,16},{24,20},{28,24},{0,28},{5,1},{9... | collective-permute-start | bytes 24584 | tf_op jit(solution)/shard_map/ppermute | solution.py:18
  13.6 6.3 %collective-permute-start.2 = (bf16[6,1,1024]{2,1,0:T(2,128)(2,1)S(1)}, bf16[6,1,1024]{2,1,0:T(2,128)(2,1)S(1)}, u32[]{:S(2)}, u32[]{:S(2)}) collective-permute-start(bf16[6,1,1024]{2,1,0:T(2,128)(2,1)S(1)} %get-tuple-element.131), channel_id=1, source_target_pairs={{0,1},{1,2},{2,3},{3,0},{4,5},{5,6},{6,7},{7,4},{8,9},{9,10},{10,1... | collective-permute-start | bytes 36872 | tf_op jit(solution)/shard_map/ppermute | solution.py:16
  15.9 4.1 %collective-permute-start.3 = (bf16[6,1,1024]{2,1,0:T(2,128)(2,1)S(1)}, bf16[6,1,1024]{2,1,0:T(2,128)(2,1)S(1)}, u32[]{:S(2)}, u32[]{:S(2)}) collective-permute-start(bf16[6,1,1024]{2,1,0:T(2,128)(2,1)S(1)} %get-tuple-element.132), channel_id=1, source_target_pairs={{1,0},{2,1},{3,2},{0,3},{5,4},{6,5},{7,6},{4,7},{9,8},{10,9},{11,1... | collective-permute-start | bytes 36872 | tf_op jit(solution)/shard_map/ppermute | solution.py:18
  20.2 1.0 copy-start.4
  24.5 2.1 copy-start.9
  27.9 4.3 %collective-permute-start.4 = (bf16[1,8,2048]{2,1,0:T(8,128)(2,1)S(1)}, bf16[1,8,2048]{2,1,0:T(8,128)(2,1)S(1)}, u32[]{:S(2)}, u32[]{:S(2)}) collective-permute-start(bf16[1,8,2048]{2,1,0:T(8,128)(2,1)S(1)} %slice.863), channel_id=1, source_target_pairs={{0,4},{4,8},{8,12},{12,16},{16,20},{20,24},{24,28},{28,0},{1,5},{5... | collective-permute-start | bytes 98312 | tf_op jit(solution)/shard_map/ppermute | solution.py:16
  28.8 8.9 %copy-start.1 = (bf16[27,64,64]{2,1,0:T(8,128)(2,1)S(1)}, bf16[27,64,64]{2,1,0:T(8,128)(2,1)}, u32[]{:S(2)}) copy-start(bf16[27,64,64]{2,1,0:T(8,128)(2,1)} %param.12) | copy-start | bytes 663556
  29.2 9.2 %copy-start.8 = (f32[64]{0:T(128)S(1)}, f32[64]{0:T(128)}, u32[]{:S(2)}) copy-start(f32[64]{0:T(128)} %param.13) | copy-start | bytes 772
  29.4 4.3 %collective-permute-start.5 = (bf16[1,8,2048]{2,1,0:T(8,128)(2,1)S(1)}, bf16[1,8,2048]{2,1,0:T(8,128)(2,1)S(1)}, u32[]{:S(2)}, u32[]{:S(2)}) collective-permute-start(bf16[1,8,2048]{2,1,0:T(8,128)(2,1)S(1)} %slice.865), channel_id=1, source_target_pairs={{4,0},{8,4},{12,8},{16,12},{20,16},{24,20},{28,24},{0,28},{5,1},{9... | collective-permute-start | bytes 98312 | tf_op jit(solution)/shard_map/ppermute | solution.py:18
  33.8 6.7 %collective-permute-start.6 = (bf16[10,1,2048]{2,1,0:T(2,128)(2,1)S(1)}, bf16[10,1,2048]{2,1,0:T(2,128)(2,1)S(1)}, u32[]{:S(2)}, u32[]{:S(2)}) collective-permute-start(bf16[10,1,2048]{2,1,0:T(2,128)(2,1)S(1)} %get-tuple-element.70), channel_id=1, source_target_pairs={{0,1},{1,2},{2,3},{3,0},{4,5},{5,6},{6,7},{7,4},{8,9},{9,10},{10,1... | collective-permute-start | bytes 122888 | tf_op jit(solution)/shard_map/ppermute | solution.py:16
  35.1 6.0 %collective-permute-start.7 = (bf16[10,1,2048]{2,1,0:T(2,128)(2,1)S(1)}, bf16[10,1,2048]{2,1,0:T(2,128)(2,1)S(1)}, u32[]{:S(2)}, u32[]{:S(2)}) collective-permute-start(bf16[10,1,2048]{2,1,0:T(2,128)(2,1)S(1)} %get-tuple-element.71), channel_id=1, source_target_pairs={{1,0},{2,1},{3,2},{0,3},{5,4},{6,5},{7,6},{4,7},{9,8},{10,9},{11,1... | collective-permute-start | bytes 122888 | tf_op jit(solution)/shard_map/ppermute | solution.py:18
  70.9 4.3 %collective-permute-start.8 = (bf16[1,8,2048]{2,1,0:T(8,128)(2,1)S(1)}, bf16[1,8,2048]{2,1,0:T(8,128)(2,1)S(1)}, u32[]{:S(2)}, u32[]{:S(2)}) collective-permute-start(bf16[1,8,2048]{2,1,0:T(8,128)(2,1)S(1)} %slice.923), channel_id=1, source_target_pairs={{0,4},{4,8},{8,12},{12,16},{16,20},{20,24},{24,28},{28,0},{1,5},{5... | collective-permute-start | bytes 98312 | tf_op jit(solution)/shard_map/ppermute | solution.py:16
  71.1 4.3 %collective-permute-start.9 = (bf16[1,8,2048]{2,1,0:T(8,128)(2,1)S(1)}, bf16[1,8,2048]{2,1,0:T(8,128)(2,1)S(1)}, u32[]{:S(2)}, u32[]{:S(2)}) collective-permute-start(bf16[1,8,2048]{2,1,0:T(8,128)(2,1)S(1)} %slice.925), channel_id=1, source_target_pairs={{4,0},{8,4},{12,8},{16,12},{20,16},{24,20},{28,24},{0,28},{5,1},{9... | collective-permute-start | bytes 98312 | tf_op jit(solution)/shard_map/ppermute | solution.py:18
  75.5 7.1 %collective-permute-start.10 = (bf16[10,1,2048]{2,1,0:T(2,128)(2,1)S(1)}, bf16[10,1,2048]{2,1,0:T(2,128)(2,1)S(1)}, u32[]{:S(2)}, u32[]{:S(2)}) collective-permute-start(bf16[10,1,2048]{2,1,0:T(2,128)(2,1)S(1)} %get-tuple-element.68), channel_id=1, source_target_pairs={{0,1},{1,2},{2,3},{3,0},{4,5},{5,6},{6,7},{7,4},{8,9},{9,10},{10,1... | collective-permute-start | bytes 122888 | tf_op jit(solution)/shard_map/ppermute | solution.py:16
  76.8 5.8 %collective-permute-start.11 = (bf16[10,1,2048]{2,1,0:T(2,128)(2,1)S(1)}, bf16[10,1,2048]{2,1,0:T(2,128)(2,1)S(1)}, u32[]{:S(2)}, u32[]{:S(2)}) collective-permute-start(bf16[10,1,2048]{2,1,0:T(2,128)(2,1)S(1)} %get-tuple-element.69), channel_id=1, source_target_pairs={{1,0},{2,1},{3,2},{0,3},{5,4},{6,5},{7,6},{4,7},{9,8},{10,9},{11,1... | collective-permute-start | bytes 122888 | tf_op jit(solution)/shard_map/ppermute | solution.py:18
  87.7 1.0 copy-start.2
  96.6 0.9 copy-start.7
  102.9 4.2 %collective-permute-start.12 = (bf16[1,4,1024]{2,1,0:T(4,128)(2,1)S(1)}, bf16[1,4,1024]{2,1,0:T(4,128)(2,1)S(1)}, u32[]{:S(2)}, u32[]{:S(2)}) collective-permute-start(bf16[1,4,1024]{2,1,0:T(4,128)(2,1)S(1)} %slice.983), channel_id=1, source_target_pairs={{0,4},{4,8},{8,12},{12,16},{16,20},{20,24},{24,28},{28,0},{1,5},{5... | collective-permute-start | bytes 24584 | tf_op jit(solution)/shard_map/ppermute | solution.py:16
  104.4 4.0 %collective-permute-start.13 = (bf16[1,4,1024]{2,1,0:T(4,128)(2,1)S(1)}, bf16[1,4,1024]{2,1,0:T(4,128)(2,1)S(1)}, u32[]{:S(2)}, u32[]{:S(2)}) collective-permute-start(bf16[1,4,1024]{2,1,0:T(4,128)(2,1)S(1)} %slice.985), channel_id=1, source_target_pairs={{4,0},{8,4},{12,8},{16,12},{20,16},{24,20},{28,24},{0,28},{5,1},{9... | collective-permute-start | bytes 24584 | tf_op jit(solution)/shard_map/ppermute | solution.py:18
  108.4 5.7 %collective-permute-start.14 = (bf16[6,1,1024]{2,1,0:T(2,128)(2,1)S(1)}, bf16[6,1,1024]{2,1,0:T(2,128)(2,1)S(1)}, u32[]{:S(2)}, u32[]{:S(2)}) collective-permute-start(bf16[6,1,1024]{2,1,0:T(2,128)(2,1)S(1)} %get-tuple-element.129), channel_id=1, source_target_pairs={{0,1},{1,2},{2,3},{3,0},{4,5},{5,6},{6,7},{7,4},{8,9},{9,10},{10,1... | collective-permute-start | bytes 36872 | tf_op jit(solution)/shard_map/ppermute | solution.py:16
  109.2 4.9 %collective-permute-start.15 = (bf16[6,1,1024]{2,1,0:T(2,128)(2,1)S(1)}, bf16[6,1,1024]{2,1,0:T(2,128)(2,1)S(1)}, u32[]{:S(2)}, u32[]{:S(2)}) collective-permute-start(bf16[6,1,1024]{2,1,0:T(2,128)(2,1)S(1)} %get-tuple-element.130), channel_id=1, source_target_pairs={{1,0},{2,1},{3,2},{0,3},{5,4},{6,5},{7,6},{4,7},{9,8},{10,9},{11,1... | collective-permute-start | bytes 36872 | tf_op jit(solution)/shard_map/ppermute | solution.py:18
  114.4 1.0 copy-start.3
  246.6 2.3 copy-start.6
  246.6 3.0 %copy-start.5 = (f32[27,64,64]{2,1,0:T(8,128)S(1)}, f32[27,64,64]{2,1,0:T(8,128)}, u32[]{:S(2)}) copy-start(f32[27,64,64]{2,1,0:T(8,128)} %get-tuple-element.141) | copy-start | bytes 1327108
Sparse Core Ops, SparseCore 0:
  113.6 132.9 all-reduce.6
where the time goes:
time: 258 us; the launch traced here: 257 us
  waiting for transfers between devices  138 us (53%)
  matrix products  41.1 us (16%)
  local copies, waits for them, and re-layouts  28.3 us (11%)
  starting transfers between devices  27.9 us (11%)
  between operations  15.8 us (6%)
  other arithmetic  6.67 us (3%)
    psum x1, waiting for transfers between devices, per_device(): lax.psum((first_term, upper_term, second_term * fine_scale), ('gx', 'gy'))  126 us
    dot_general x108, matrix products, conv_local(): jnp.dot(piece, weights[k], preferred_element_type=jnp.float32)  26.5 us
    ppermute x8, starting transfers between devices, extended(): lax.ppermute(head, axis, [((i + 1) % count, i) for i in range(count)])  21.1 us
    dot_general x54, matrix products, wgrad_local(): lax.dot_general(piece, flat_grad, (((0,), (0,)), ((), ())), preferred_ele...  13.7 us
    slice x8, local copies, waits for them, and re-layouts, conv_local(): piece = padded[ox:ox + rows, oy:oy + cols, oz:oz + depth].reshape(-1, chans)  10.6 us
    ppermute x8, waiting for transfers between devices, extended(): lax.ppermute(tail, axis, [(i, (i + 1) % count) for i in range(count)])  7.88 us
    ppermute x8, starting transfers between devices, extended(): lax.ppermute(tail, axis, [(i, (i + 1) % count) for i in range(count)])  6.77 us
    unnamed x29, local copies, waits for them, and re-layouts  6.38 us
  transfers between devices with their start and end apart: 17, of which 14 were waited for; matrix products, arithmetic and copies ran while one was open for 5% of the time, Pallas kernels for 0%

commit v1 on v0

--- a/solution.py
+++ b/solution.py
@@ -1,8 +1,11 @@
+import functools
 import math
 
 import jax
 import jax.numpy as jnp
 from jax import lax
+from jax.experimental import pallas as pl
+from jax.experimental.pallas import tpu as pltpu
 from jax.sharding import PartitionSpec as P
 
 
@@ -68,6 +71,121 @@
     rows, cols, depth, chans = hidden.shape
     fine = jnp.einsum("xyze,abced->xaybzcd", hidden, upper_taps, preferred_element_type=jnp.float32)
     return fine.reshape(2 * rows, 2 * cols, 2 * depth, chans).astype(jnp.bfloat16)
+
+
+MESH = pl.DeviceIdType.MESH
+
+
+def add_up(nx, ny, part, full, first_in, line, line_in, sems):
+    mx, my = lax.axis_index("gx"), lax.axis_index("gy")
+    rows = part.shape[0] // nx
+    small = rows // ny
+    s1, r1, s2, r2, s3, r3, s4, r4 = sems
+
+    def chunk(i):
+        return pl.ds(pl.multiple_of(i * rows, 16), rows)
+
+    def piece(i):
+        return pl.ds(pl.multiple_of(i * small, 16), small)
+
+    def along_x(d):
+        return lax.rem(mx + d, nx)
+
+    def along_y(d):
+        return lax.rem(my + d, ny)
+
+    def spread(copies):
+        for copy in copies:
+            copy.start()
+        return copies
+
+    def finish(copies):
+        for copy in copies:
+            copy.wait()
+
+    finish(spread([
+        pltpu.make_async_remote_copy(
+            src_ref=part.at[chunk(along_x(d))], dst_ref=first_in.at[d - 1],
+            send_sem=s1.at[d - 1], recv_sem=r1.at[d - 1],
+            device_id=(along_x(d), my), device_id_type=MESH)
+        for d in range(1, nx)
+    ]))
+    total = part[chunk(mx), :].astype(jnp.float32)
+    for d in range(nx - 1):
+        total += first_in[d].astype(jnp.float32)
+    line[...] = total.astype(jnp.bfloat16)
+    finish(spread([
+        pltpu.make_async_remote_copy(
+            src_ref=line.at[piece(along_y(d))], dst_ref=line_in.at[d - 1],
+            send_sem=s2.at[d - 1], recv_sem=r2.at[d - 1],
+            device_id=(mx, along_y(d)), device_id_type=MESH)
+        for d in range(1, ny)
+    ]))
+    total = line[piece(my), :].astype(jnp.float32)
+    for d in range(ny - 1):
+        total += line_in[d].astype(jnp.float32)
+    mine = pl.ds(pl.multiple_of(mx * rows + my * small, 16), small)
+    full[mine, :] = total.astype(jnp.bfloat16)
+    finish(spread([
+        pltpu.make_async_remote_copy(
+            src_ref=full.at[mine], dst_ref=full.at[mine],
+            send_sem=s3.at[d - 1], recv_sem=r3.at[d - 1],
+            device_id=(mx, along_y(d)), device_id_type=MESH)
+        for d in range(1, ny)
+    ]))
+    finish(spread([
+        pltpu.make_async_remote_copy(
+            src_ref=full.at[chunk(mx)], dst_ref=full.at[chunk(mx)],
+            send_sem=s4.at[d - 1], recv_sem=r4.at[d - 1],
+            device_id=(along_x(d), my), device_id_type=MESH)
+        for d in range(1, nx)
+    ]))
+
+
+def add_up_scratch(nx, ny, height):
+    dma = pltpu.SemaphoreType.DMA
+    rows = height // nx
+    return [
+        pltpu.VMEM((nx - 1, rows, 128), jnp.bfloat16),
+        pltpu.VMEM((rows, 128), jnp.bfloat16),
+        pltpu.VMEM((ny - 1, rows // ny, 128), jnp.bfloat16),
+        dma((nx - 1,)), dma((nx - 1,)), dma((ny - 1,)), dma((ny - 1,)),
+        dma((ny - 1,)), dma((ny - 1,)), dma((nx - 1,)), dma((nx - 1,)),
+    ]
+
+
+def sum_kernel(nx, ny, part, out, full, first_in, line, line_in, *sems):
+    mx, my = lax.axis_index("gx"), lax.axis_index("gy")
+    barrier = pltpu.get_barrier_semaphore()
+    for d in range(1, nx):
+        pl.semaphore_signal(barrier, inc=1, device_id=(lax.rem(mx + d, nx), my), device_id_type=MESH)
+    for d in range(1, ny):
+        pl.semaphore_signal(barrier, inc=1, device_id=(mx, lax.rem(my + d, ny)), device_id_type=MESH)
+    pl.semaphore_wait(barrier, nx + ny - 2)
+    add_up(nx, ny, part, full, first_in, line, line_in, sems)
+    out[...] = full[...].astype(jnp.float32)
+
+
+def sum_all(terms):
+    nx, ny = lax.axis_size("gx"), lax.axis_size("gy")
+    unit = 16 * nx * ny
+    flat = jnp.concatenate([t.reshape(-1, 128) for t in terms]).astype(jnp.bfloat16)
+    height = -(-flat.shape[0] // unit) * unit
+    flat = jnp.pad(flat, ((0, height - flat.shape[0]), (0, 0)))
+    total = pl.pallas_call(
+        functools.partial(sum_kernel, nx, ny),
+        out_shape=jax.ShapeDtypeStruct((height, 128), jnp.float32),
+        in_specs=[pl.BlockSpec(memory_space=pltpu.VMEM)],
+        out_specs=pl.BlockSpec(memory_space=pltpu.VMEM),
+        scratch_shapes=[pltpu.VMEM((height, 128), jnp.bfloat16)] + add_up_scratch(nx, ny, height),
+        compiler_params=pltpu.CompilerParams(collective_id=0, has_side_effects=True, vmem_limit_bytes=32 << 20),
+    )(flat)
+    outs, at = [], 0
+    for t in terms:
+        size = t.size // 128
+        outs.append(total[at : at + size].reshape(t.shape))
+        at += size
+    return outs
 
 
 def per_device(field_in, w_first, b_first, w_upper, w_second, b_second, cotangent, tile_weights):
@@ -111,9 +229,7 @@
     grad_input = conv_local(coarse_pad, flip_taps(w_first), rows, cols).astype(jnp.bfloat16)
     second_term = wgrad_local(upper_pad, grad_pre)
     first_term = wgrad_local(input_pad, grad_pre_first) * coarse_scale
-    grad_first, grad_upper, grad_second = lax.psum(
-        (first_term, upper_term, second_term * fine_scale), ("gx", "gy")
-    )
+    grad_first, grad_upper, grad_second = sum_all((first_term, upper_term, second_term * fine_scale))
     return (
         output_field.reshape(2 * rows, 2 * cols, 2 * flat),
         grad_input.reshape(rows, cols, flat),

time: 258 us -> 134 us (0.52)
  waiting for transfers between devices: 138 us -> 9.35 us
  Pallas kernels: 0 us -> 22.9 us
  between operations: 15.8 us -> 2.58 us
    psum x1 -> x0, waiting for transfers between devices: 126 us -> none  [per_device(): lax.psum((first_term, upper_term, second_term * fine_scale), ('gx', 'gy'))]
    pallas_call x0 -> x1, Pallas kernels: none -> 22.9 us  [sum_all(): pl.pallas_call(functools.partial(sum_kernel, nx, ny), out_shape=jax.Shape...]
    unnamed x29 -> x22, local copies, waits for them, and re-layouts: 6.38 us -> 2.34 us
    reshape x0 -> x3, local copies, waits for them, and re-layouts: none -> 3.04 us  [sum_all(): outs.append(total[at:at + size].reshape(t.shape))]
  transfers between devices with their start and end apart: 17 -> 16, of which waited for: 14 -> 9; matrix products, arithmetic and copies ran while one was open for 5% -> 15% of each run, Pallas kernels for 0% -> 17%
where the time goes in v1:
time: 134 us
  matrix products  40.9 us (31%)
  local copies, waits for them, and re-layouts  27 us (20%)
  starting transfers between devices  26.3 us (20%)
  Pallas kernels  22.9 us (17%)
  waiting for transfers between devices  9.35 us (7%)
  other arithmetic  4.9 us (4%)
  between operations  2.58 us (2%)
    dot_general x108, matrix products, conv_local(): jnp.dot(piece, weights[k], preferred_element_type=jnp.float32)  26.5 us
    pallas_call x1, Pallas kernels, sum_all(): pl.pallas_call(functools.partial(sum_kernel, nx, ny), out_shape=jax.Shape...  22.9 us
    ppermute x8, starting transfers between devices, extended(): lax.ppermute(head, axis, [((i + 1) % count, i) for i in range(count)])  19.8 us
    dot_general x54, matrix products, wgrad_local(): lax.dot_general(piece, flat_grad, (((0,), (0,)), ((), ())), preferred_ele...  13.5 us
    slice x8, local copies, waits for them, and re-layouts, conv_local(): piece = padded[ox:ox + rows, oy:oy + cols, oz:oz + depth].reshape(-1, chans)  10.4 us
    ppermute x8, starting transfers between devices, extended(): lax.ppermute(tail, axis, [(i, (i + 1) % count) for i in range(count)])  6.49 us
    ppermute x8, waiting for transfers between devices, extended(): lax.ppermute(tail, axis, [(i, (i + 1) % count) for i in range(count)])  6.3 us
    convert_element_type x2, other arithmetic, per_device(): grad_pre = (weight_grid * fine_cot * slope_fine).reshape(2 * rows, 2 * co...  3.75 us
  transfers between devices with their start and end apart: 16, of which 9 were waited for; matrix products, arithmetic and copies ran while one was open for 15% of the time, Pallas kernels for 17%

profile of v1, /device:TPU:0, one launch (start us, length us, event | category | flops | bytes accessed | tf_op | source)
XLA Modules:
  0.0 133.8 jit_solution(6398115847989097034)
XLA Ops:
  0.6 0.8 fusion.197
  1.4 0.5 collective-permute-start
  1.9 2.9 %collective-permute-start.1 = (bf16[1,4,1024]{2,1,0:T(4,128)(2,1)S(1)}, bf16[1,4,1024]{2,1,0:T(4,128)(2,1)S(1)}, u32[]{:S(2)}, u32[]{:S(2)}) collective-permute-start(bf16[1,4,1024]{2,1,0:T(4,128)(2,1)S(1)} %get-tuple-element.132), channel_id=1, source_target_pairs={{4,0},{8,4},{12,8},{16,12},{20,16},{24,20},{28,24},{0,28},{5,1},{9... | collective-permute-start | bytes 24584 | tf_op jit(solution)/shard_map/ppermute | solution.py:21
  4.9 1.3 collective-permute-done
  6.1 0.8 constant_dynamic-update-slice_fusion.1
  7.0 2.4 %collective-permute-start.2 = (bf16[6,1,1024]{2,1,0:T(2,128)(2,1)S(1)}, bf16[6,1,1024]{2,1,0:T(2,128)(2,1)S(1)}, u32[]{:S(2)}, u32[]{:S(2)}) collective-permute-start(bf16[6,1,1024]{2,1,0:T(2,128)(2,1)S(1)} %get-tuple-element.130), channel_id=1, source_target_pairs={{0,1},{1,2},{2,3},{3,0},{4,5},{5,6},{6,7},{7,4},{8,9},{9,10},{10,1... | collective-permute-start | bytes 36872 | tf_op jit(solution)/shard_map/ppermute | solution.py:19
  9.4 2.1 %collective-permute-start.3 = (bf16[6,1,1024]{2,1,0:T(2,128)(2,1)S(1)}, bf16[6,1,1024]{2,1,0:T(2,128)(2,1)S(1)}, u32[]{:S(2)}, u32[]{:S(2)}) collective-permute-start(bf16[6,1,1024]{2,1,0:T(2,128)(2,1)S(1)} %get-tuple-element.131), channel_id=1, source_target_pairs={{1,0},{2,1},{3,2},{0,3},{5,4},{6,5},{7,6},{4,7},{9,8},{10,9},{11,1... | collective-permute-start | bytes 36872 | tf_op jit(solution)/shard_map/ppermute | solution.py:21
  11.5 1.8 %collective-permute-done.2 = bf16[6,1,1024]{2,1,0:T(2,128)(2,1)S(1)} collective-permute-done((bf16[6,1,1024]{2,1,0:T(2,128)(2,1)S(1)}, bf16[6,1,1024]{2,1,0:T(2,128)(2,1)S(1)}, u32[]{:S(2)}, u32[]{:S(2)}) %collective-permute-start.2) | collective-permute-done | bytes 12320 | tf_op jit(solution)/shard_map/ppermute | solution.py:19
  13.8 0.3 pad_slice_fusion.54
  14.1 0.6 copy-done.4
  20.7 0.5 copy.21
  21.4 0.8 reverse_bitcast_fusion
  22.2 0.5 convert_element_type.68
  22.8 2.7 %collective-permute-start.5 = (bf16[1,8,2048]{2,1,0:T(8,128)(2,1)S(1)}, bf16[1,8,2048]{2,1,0:T(8,128)(2,1)S(1)}, u32[]{:S(2)}, u32[]{:S(2)}) collective-permute-start(bf16[1,8,2048]{2,1,0:T(8,128)(2,1)S(1)} %slice.874), channel_id=1, source_target_pairs={{4,0},{8,4},{12,8},{16,12},{20,16},{24,20},{28,24},{0,28},{5,1},{9... | collective-permute-start | bytes 98312 | tf_op jit(solution)/shard_map/ppermute | solution.py:21
  25.7 1.4 %collective-permute-done.5 = bf16[1,8,2048]{2,1,0:T(8,128)(2,1)S(1)} collective-permute-done((bf16[1,8,2048]{2,1,0:T(8,128)(2,1)S(1)}, bf16[1,8,2048]{2,1,0:T(8,128)(2,1)S(1)}, u32[]{:S(2)}, u32[]{:S(2)}) %collective-permute-start.5) | collective-permute-done | bytes 32800 | tf_op jit(solution)/shard_map/ppermute | solution.py:21
  27.2 1.4 %collective-permute-start.6 = (bf16[10,1,2048]{2,1,0:T(2,128)(2,1)S(1)}, bf16[10,1,2048]{2,1,0:T(2,128)(2,1)S(1)}, u32[]{:S(2)}, u32[]{:S(2)}) collective-permute-start(bf16[10,1,2048]{2,1,0:T(2,128)(2,1)S(1)} %get-tuple-element.69), channel_id=1, source_target_pairs={{0,1},{1,2},{2,3},{3,0},{4,5},{5,6},{6,7},{7,4},{8,9},{9,10},{10,1... | collective-permute-start | bytes 122888 | tf_op jit(solution)/shard_map/ppermute | solution.py:19
  28.6 2.6 %collective-permute-start.7 = (bf16[10,1,2048]{2,1,0:T(2,128)(2,1)S(1)}, bf16[10,1,2048]{2,1,0:T(2,128)(2,1)S(1)}, u32[]{:S(2)}, u32[]{:S(2)}) collective-permute-start(bf16[10,1,2048]{2,1,0:T(2,128)(2,1)S(1)} %get-tuple-element.70), channel_id=1, source_target_pairs={{1,0},{2,1},{3,2},{0,3},{5,4},{6,5},{7,6},{4,7},{9,8},{10,9},{11,1... | collective-permute-start | bytes 122888 | tf_op jit(solution)/shard_map/ppermute | solution.py:21
  31.1 0.8 reverse_bitcast_fusion.1
  32.7 0.8 copy.27
  33.4 0.5 collective-permute-done.6
  33.9 0.6 collective-permute-done.7
  34.8 0.8 reshape.513
  35.6 0.8 fusion.188
  36.5 3.9 %pad_slice_fusion.18 = (bf16[8,8,32,64]{3,2,1,0:T(8,128)(2,1)S(1)}, bf16[8,8,32,64]{3,2,1,0:T(8,128)(2,1)S(1)}, bf16[8,8,32,64]{3,2,1,0:T(8,128)(2,1)S(1)}, bf16...) fusion(bf16[10,10,32,64]{3,2,1,0:T(8,128)(2,1)S(1)} %reshape.513), kind=kLoop, calls=%fused_computation.250 | loop fusion | bytes 6848512 | tf_op jit(solution)/shard_map/slice | solution.py:46
  44.8 0.3 convolution_add_fusion.39
  48.5 0.3 convolution_add_fusion.28
  49.9 0.4 reshape.541
  50.2 2.2 %multiply_convert_fusion.3 = (bf16[8,8,2048]{2,1,0:T(8,128)(2,1)S(1)}, bf16[8,8,2048]{2,1,0:T(8,128)(2,1)}, f32[8,8,2048]{2,1,0:T(8,128)S(1)}) fusion(f32[8,8,2048]{2,1,0:T(8,128)S(1)} %reshape.541, f32[2048]{0:T(1024)S(1)} %add.455, bf16[8,8,2048]{2,1,0:T(8,128)(2,1)} %param.14, f32[]{:T(128)} %bitcast.116), kind=kLoop, calls=%fused_computation.275 | loop fusion | flops 2621440 | bytes 1843204 | tf_op jit(solution)/shard_map/convert_element_type | solution.py:214
  52.4 1.4 %mul.98 = f32[8,8,32,64]{3,2,1,0:T(8,128)} reshape(f32[8,8,2048]{2,1,0:T(8,128)S(1)} %get-tuple-element.71) | data formatting | bytes 1048576 | tf_op jit(solution)/shard_map/mul | solution.py:212
  53.8 1.6 %multiply_convert_fusion = bf16[8,8,32,64]{3,2,1,0:T(8,128)(2,1)S(1)} fusion(f32[8,8,32,64]{3,2,1,0:T(8,128)} %mul.98, f32[8,8,32,64]{3,2,1,0:T(8,128)S(1)} %bitcast.1111, f32[64]{0:T(128)S(1)} %copy-done.6), kind=kLoop, calls=%fused_computation.229 | loop fusion | flops 1048576 | bytes 1310976 | tf_op jit(solution)/shard_map/convert_element_type | solution.py:214
  56.0 1.3 collective-permute-start.9
  65.9 1.3 collective-permute-start.10
  67.2 2.6 %collective-permute-start.11 = (bf16[10,1,2048]{2,1,0:T(2,128)(2,1)S(1)}, bf16[10,1,2048]{2,1,0:T(2,128)(2,1)S(1)}, u32[]{:S(2)}, u32[]{:S(2)}) collective-permute-start(bf16[10,1,2048]{2,1,0:T(2,128)(2,1)S(1)} %get-tuple-element.68), channel_id=1, source_target_pairs={{1,0},{2,1},{3,2},{0,3},{5,4},{6,5},{7,6},{4,7},{9,8},{10,9},{11,1... | collective-permute-start | bytes 122888 | tf_op jit(solution)/shard_map/ppermute | solution.py:21
  70.1 2.6 %collective-permute-done.10 = bf16[10,1,2048]{2,1,0:T(2,128)(2,1)S(1)} collective-permute-done((bf16[10,1,2048]{2,1,0:T(2,128)(2,1)S(1)}, bf16[10,1,2048]{2,1,0:T(2,128)(2,1)S(1)}, u32[]{:S(2)}, u32[]{:S(2)}) %collective-permute-start.10) | collective-permute-done | bytes 40992 | tf_op jit(solution)/shard_map/ppermute | solution.py:19
  72.7 0.8 collective-permute-done.11
  73.8 0.8 reshape.543
  74.6 0.8 fusion.187
  75.5 3.9 %pad_slice_fusion = (bf16[8,8,32,64]{3,2,1,0:T(8,128)(2,1)S(1)}, bf16[8,8,32,64]{3,2,1,0:T(8,128)(2,1)S(1)}, bf16[8,8,32,64]{3,2,1,0:T(8,128)(2,1)S(1)}, bf16[8,...) fusion(bf16[10,10,32,64]{3,2,1,0:T(8,128)(2,1)S(1)} %reshape.543), kind=kLoop, calls=%fused_computation.232 | loop fusion | bytes 6848512 | tf_op jit(solution)/shard_map/slice | solution.py:46
  89.7 2.6 %collective-permute-start.13 = (bf16[1,4,1024]{2,1,0:T(4,128)(2,1)S(1)}, bf16[1,4,1024]{2,1,0:T(4,128)(2,1)S(1)}, u32[]{:S(2)}, u32[]{:S(2)}) collective-permute-start(bf16[1,4,1024]{2,1,0:T(4,128)(2,1)S(1)} %slice.994), channel_id=1, source_target_pairs={{4,0},{8,4},{12,8},{16,12},{20,16},{24,20},{28,24},{0,28},{5,1},{9... | collective-permute-start | bytes 24584 | tf_op jit(solution)/shard_map/ppermute | solution.py:21
  97.5 22.9 %shard_map.119 = f32[2048,128]{1,0:T(8,128)S(1)} custom-call(bf16[2048,128]{1,0:T(8,128)(2,1)S(1)} %fusion.67.part), custom_call_target="tpu_custom_call" | custom-call | tf_op jit(solution)/shard_map/pallas_call | solution.py:175
  120.5 0.8 collective-permute-start.14
  121.3 3.0 %collective-permute-start.15 = (bf16[6,1,1024]{2,1,0:T(2,128)(2,1)S(1)}, bf16[6,1,1024]{2,1,0:T(2,128)(2,1)S(1)}, u32[]{:S(2)}, u32[]{:S(2)}) collective-permute-start(bf16[6,1,1024]{2,1,0:T(2,128)(2,1)S(1)} %get-tuple-element.129), channel_id=1, source_target_pairs={{1,0},{2,1},{3,2},{0,3},{5,4},{6,5},{7,6},{4,7},{9,8},{10,9},{11,1... | collective-permute-start | bytes 36872 | tf_op jit(solution)/shard_map/ppermute | solution.py:21
  124.4 0.8 reshape.602
  125.2 1.1 reshape.603
  126.4 1.1 reshape.601
  127.8 0.3 pad_slice_fusion.36
  128.1 0.6 copy-done.3
  133.1 0.7 convert_element_type.76
  (234 shorter events, 45.3 us)
Async XLA Ops:
  0.6 19.7 %copy-start = (bf16[8,64,64]{2,1,0:T(8,128)(2,1)S(1)}, bf16[8,64,64]{2,1,0:T(8,128)(2,1)}, u32[]{:S(2)}) copy-start(bf16[8,64,64]{2,1,0:T(8,128)(2,1)} %param.11) | copy-start | bytes 196612
  1.4 4.7 %collective-permute-start = (bf16[1,4,1024]{2,1,0:T(4,128)(2,1)S(1)}, bf16[1,4,1024]{2,1,0:T(4,128)(2,1)S(1)}, u32[]{:S(2)}, u32[]{:S(2)}) collective-permute-start(bf16[1,4,1024]{2,1,0:T(4,128)(2,1)S(1)} %get-tuple-element.133), channel_id=1, source_target_pairs={{0,4},{4,8},{8,12},{12,16},{16,20},{20,24},{24,28},{28,0},{1,5},{5... | collective-permute-start | bytes 24584 | tf_op jit(solution)/shard_map/ppermute | solution.py:19
  1.9 5.0 %collective-permute-start.1 = (bf16[1,4,1024]{2,1,0:T(4,128)(2,1)S(1)}, bf16[1,4,1024]{2,1,0:T(4,128)(2,1)S(1)}, u32[]{:S(2)}, u32[]{:S(2)}) collective-permute-start(bf16[1,4,1024]{2,1,0:T(4,128)(2,1)S(1)} %get-tuple-element.132), channel_id=1, source_target_pairs={{4,0},{8,4},{12,8},{16,12},{20,16},{24,20},{28,24},{0,28},{5,1},{9... | collective-permute-start | bytes 24584 | tf_op jit(solution)/shard_map/ppermute | solution.py:21
  7.0 6.3 %collective-permute-start.2 = (bf16[6,1,1024]{2,1,0:T(2,128)(2,1)S(1)}, bf16[6,1,1024]{2,1,0:T(2,128)(2,1)S(1)}, u32[]{:S(2)}, u32[]{:S(2)}) collective-permute-start(bf16[6,1,1024]{2,1,0:T(2,128)(2,1)S(1)} %get-tuple-element.130), channel_id=1, source_target_pairs={{0,1},{1,2},{2,3},{3,0},{4,5},{5,6},{6,7},{7,4},{8,9},{9,10},{10,1... | collective-permute-start | bytes 36872 | tf_op jit(solution)/shard_map/ppermute | solution.py:19
  9.4 4.1 %collective-permute-start.3 = (bf16[6,1,1024]{2,1,0:T(2,128)(2,1)S(1)}, bf16[6,1,1024]{2,1,0:T(2,128)(2,1)S(1)}, u32[]{:S(2)}, u32[]{:S(2)}) collective-permute-start(bf16[6,1,1024]{2,1,0:T(2,128)(2,1)S(1)} %get-tuple-element.131), channel_id=1, source_target_pairs={{1,0},{2,1},{3,2},{0,3},{5,4},{6,5},{7,6},{4,7},{9,8},{10,9},{11,1... | collective-permute-start | bytes 36872 | tf_op jit(solution)/shard_map/ppermute | solution.py:21
  13.7 1.0 copy-start.4
  17.9 2.1 %copy-start.7 = (f32[64]{0:T(128)S(1)}, f32[64]{0:T(128)}, u32[]{:S(2)}) copy-start(f32[64]{0:T(128)} %param.10) | copy-start | bytes 772
  21.3 4.3 %collective-permute-start.4 = (bf16[1,8,2048]{2,1,0:T(8,128)(2,1)S(1)}, bf16[1,8,2048]{2,1,0:T(8,128)(2,1)S(1)}, u32[]{:S(2)}, u32[]{:S(2)}) collective-permute-start(bf16[1,8,2048]{2,1,0:T(8,128)(2,1)S(1)} %slice.872), channel_id=1, source_target_pairs={{0,4},{4,8},{8,12},{12,16},{16,20},{20,24},{24,28},{28,0},{1,5},{5... | collective-permute-start | bytes 98312 | tf_op jit(solution)/shard_map/ppermute | solution.py:19
  22.2 8.9 %copy-start.1 = (bf16[27,64,64]{2,1,0:T(8,128)(2,1)S(1)}, bf16[27,64,64]{2,1,0:T(8,128)(2,1)}, u32[]{:S(2)}) copy-start(bf16[27,64,64]{2,1,0:T(8,128)(2,1)} %param.12) | copy-start | bytes 663556
  22.6 9.9 %copy-start.6 = (f32[64]{0:T(128)S(1)}, f32[64]{0:T(128)}, u32[]{:S(2)}) copy-start(f32[64]{0:T(128)} %param.13) | copy-start | bytes 772
  22.8 4.3 %collective-permute-start.5 = (bf16[1,8,2048]{2,1,0:T(8,128)(2,1)S(1)}, bf16[1,8,2048]{2,1,0:T(8,128)(2,1)S(1)}, u32[]{:S(2)}, u32[]{:S(2)}) collective-permute-start(bf16[1,8,2048]{2,1,0:T(8,128)(2,1)S(1)} %slice.874), channel_id=1, source_target_pairs={{4,0},{8,4},{12,8},{16,12},{20,16},{24,20},{28,24},{0,28},{5,1},{9... | collective-permute-start | bytes 98312 | tf_op jit(solution)/shard_map/ppermute | solution.py:21
  27.2 6.7 %collective-permute-start.6 = (bf16[10,1,2048]{2,1,0:T(2,128)(2,1)S(1)}, bf16[10,1,2048]{2,1,0:T(2,128)(2,1)S(1)}, u32[]{:S(2)}, u32[]{:S(2)}) collective-permute-start(bf16[10,1,2048]{2,1,0:T(2,128)(2,1)S(1)} %get-tuple-element.69), channel_id=1, source_target_pairs={{0,1},{1,2},{2,3},{3,0},{4,5},{5,6},{6,7},{7,4},{8,9},{9,10},{10,1... | collective-permute-start | bytes 122888 | tf_op jit(solution)/shard_map/ppermute | solution.py:19
  28.6 6.0 %collective-permute-start.7 = (bf16[10,1,2048]{2,1,0:T(2,128)(2,1)S(1)}, bf16[10,1,2048]{2,1,0:T(2,128)(2,1)S(1)}, u32[]{:S(2)}, u32[]{:S(2)}) collective-permute-start(bf16[10,1,2048]{2,1,0:T(2,128)(2,1)S(1)} %get-tuple-element.70), channel_id=1, source_target_pairs={{1,0},{2,1},{3,2},{0,3},{5,4},{6,5},{7,6},{4,7},{9,8},{10,9},{11,1... | collective-permute-start | bytes 122888 | tf_op jit(solution)/shard_map/ppermute | solution.py:21
  56.0 9.7 %collective-permute-start.9 = (bf16[1,8,2048]{2,1,0:T(8,128)(2,1)S(1)}, bf16[1,8,2048]{2,1,0:T(8,128)(2,1)S(1)}, u32[]{:S(2)}, u32[]{:S(2)}) collective-permute-start(bf16[1,8,2048]{2,1,0:T(8,128)(2,1)S(1)} %slice.934), channel_id=1, source_target_pairs={{4,0},{8,4},{12,8},{16,12},{20,16},{24,20},{28,24},{0,28},{5,1},{9... | collective-permute-start | bytes 98312 | tf_op jit(solution)/shard_map/ppermute | solution.py:21
  57.3 8.4 %collective-permute-start.8 = (bf16[1,8,2048]{2,1,0:T(8,128)(2,1)S(1)}, bf16[1,8,2048]{2,1,0:T(8,128)(2,1)S(1)}, u32[]{:S(2)}, u32[]{:S(2)}) collective-permute-start(bf16[1,8,2048]{2,1,0:T(8,128)(2,1)S(1)} %slice.932), channel_id=1, source_target_pairs={{0,4},{4,8},{8,12},{12,16},{16,20},{20,24},{24,28},{28,0},{1,5},{5... | collective-permute-start | bytes 98312 | tf_op jit(solution)/shard_map/ppermute | solution.py:19
  65.9 6.8 %collective-permute-start.10 = (bf16[10,1,2048]{2,1,0:T(2,128)(2,1)S(1)}, bf16[10,1,2048]{2,1,0:T(2,128)(2,1)S(1)}, u32[]{:S(2)}, u32[]{:S(2)}) collective-permute-start(bf16[10,1,2048]{2,1,0:T(2,128)(2,1)S(1)} %get-tuple-element.67), channel_id=1, source_target_pairs={{0,1},{1,2},{2,3},{3,0},{4,5},{5,6},{6,7},{7,4},{8,9},{9,10},{10,1... | collective-permute-start | bytes 122888 | tf_op jit(solution)/shard_map/ppermute | solution.py:19
  67.2 6.3 %collective-permute-start.11 = (bf16[10,1,2048]{2,1,0:T(2,128)(2,1)S(1)}, bf16[10,1,2048]{2,1,0:T(2,128)(2,1)S(1)}, u32[]{:S(2)}, u32[]{:S(2)}) collective-permute-start(bf16[10,1,2048]{2,1,0:T(2,128)(2,1)S(1)} %get-tuple-element.68), channel_id=1, source_target_pairs={{1,0},{2,1},{3,2},{0,3},{5,4},{6,5},{7,6},{4,7},{9,8},{10,9},{11,1... | collective-permute-start | bytes 122888 | tf_op jit(solution)/shard_map/ppermute | solution.py:21
  75.5 4.0 %copy-start.2 = (bf16[27,64,64]{1,2,0:T(8,128)(2,1)S(1)}, bf16[27,64,64]{1,2,0:T(8,128)(2,1)}, u32[]{:S(2)}) copy-start(bf16[27,64,64]{1,2,0:T(8,128)(2,1)} %reverse_bitcast_fusion.1) | copy-start | bytes 663556
  87.3 0.9 copy-start.5
  89.6 30.8 %collective-permute-start.12 = (bf16[1,4,1024]{2,1,0:T(4,128)(2,1)S(1)}, bf16[1,4,1024]{2,1,0:T(4,128)(2,1)S(1)}, u32[]{:S(2)}, u32[]{:S(2)}) collective-permute-start(bf16[1,4,1024]{2,1,0:T(4,128)(2,1)S(1)} %slice.992), channel_id=1, source_target_pairs={{0,4},{4,8},{8,12},{12,16},{16,20},{20,24},{24,28},{28,0},{1,5},{5... | collective-permute-start | bytes 24584 | tf_op jit(solution)/shard_map/ppermute | solution.py:19
  89.7 30.7 %collective-permute-start.13 = (bf16[1,4,1024]{2,1,0:T(4,128)(2,1)S(1)}, bf16[1,4,1024]{2,1,0:T(4,128)(2,1)S(1)}, u32[]{:S(2)}, u32[]{:S(2)}) collective-permute-start(bf16[1,4,1024]{2,1,0:T(4,128)(2,1)S(1)} %slice.994), channel_id=1, source_target_pairs={{4,0},{8,4},{12,8},{16,12},{20,16},{24,20},{28,24},{0,28},{5,1},{9... | collective-permute-start | bytes 24584 | tf_op jit(solution)/shard_map/ppermute | solution.py:21
  120.5 7.0 %collective-permute-start.14 = (bf16[6,1,1024]{2,1,0:T(2,128)(2,1)S(1)}, bf16[6,1,1024]{2,1,0:T(2,128)(2,1)S(1)}, u32[]{:S(2)}, u32[]{:S(2)}) collective-permute-start(bf16[6,1,1024]{2,1,0:T(2,128)(2,1)S(1)} %get-tuple-element.128), channel_id=1, source_target_pairs={{0,1},{1,2},{2,3},{3,0},{4,5},{5,6},{6,7},{7,4},{8,9},{9,10},{10,1... | collective-permute-start | bytes 36872 | tf_op jit(solution)/shard_map/ppermute | solution.py:19
  121.3 6.2 %collective-permute-start.15 = (bf16[6,1,1024]{2,1,0:T(2,128)(2,1)S(1)}, bf16[6,1,1024]{2,1,0:T(2,128)(2,1)S(1)}, u32[]{:S(2)}, u32[]{:S(2)}) collective-permute-start(bf16[6,1,1024]{2,1,0:T(2,128)(2,1)S(1)} %get-tuple-element.129), channel_id=1, source_target_pairs={{1,0},{2,1},{3,2},{0,3},{5,4},{6,5},{7,6},{4,7},{9,8},{10,9},{11,1... | collective-permute-start | bytes 36872 | tf_op jit(solution)/shard_map/ppermute | solution.py:21
  127.7 1.0 copy-start.3

commit v2 on v1

v2 whole, which is shorter than its diff:
```python
import functools
import math

import jax
import jax.numpy as jnp
from jax import lax
from jax.experimental import pallas as pl
from jax.experimental.pallas import tpu as pltpu
from jax.sharding import PartitionSpec as P


MESH = pl.DeviceIdType.MESH


def add_up(nx, ny, part, full, first_in, line, line_in, sems):
    mx, my = lax.axis_index("gx"), lax.axis_index("gy")
    rows = part.shape[0] // nx
    small = rows // ny
    s1, r1, s2, r2, s3, r3, s4, r4 = sems

    def chunk(i):
        return pl.ds(pl.multiple_of(i * rows, 16), rows)

    def piece(i):
        return pl.ds(pl.multiple_of(i * small, 16), small)

    def along_x(d):
        return lax.rem(mx + d, nx)

    def along_y(d):
        return lax.rem(my + d, ny)

    def spread(copies):
        for copy in copies:
            copy.start()
        return copies

    def finish(copies):
        for copy in copies:
            copy.wait()

    finish(spread([
        pltpu.make_async_remote_copy(
            src_ref=part.at[chunk(along_x(d))], dst_ref=first_in.at[d - 1],
            send_sem=s1.at[d - 1], recv_sem=r1.at[d - 1],
            device_id=(along_x(d), my), device_id_type=MESH)
        for d in range(1, nx)
    ]))
    total = part[chunk(mx), :].astype(jnp.float32)
    for d in range(nx - 1):
        total += first_in[d].astype(jnp.float32)
    line[...] = total.astype(jnp.bfloat16)
    finish(spread([
        pltpu.make_async_remote_copy(
            src_ref=line.at[piece(along_y(d))], dst_ref=line_in.at[d - 1],
            send_sem=s2.at[d - 1], recv_sem=r2.at[d - 1],
            device_id=(mx, along_y(d)), device_id_type=MESH)
        for d in range(1, ny)
    ]))
    total = line[piece(my), :].astype(jnp.float32)
    for d in range(ny - 1):
        total += line_in[d].astype(jnp.float32)
    mine = pl.ds(pl.multiple_of(mx * rows + my * small, 16), small)
    full[mine, :] = total.astype(jnp.bfloat16)
    finish(spread([
        pltpu.make_async_remote_copy(
            src_ref=full.at[mine], dst_ref=full.at[mine],
            send_sem=s3.at[d - 1], recv_sem=r3.at[d - 1],
            device_id=(mx, along_y(d)), device_id_type=MESH)
        for d in range(1, ny)
    ]))
    finish(spread([
        pltpu.make_async_remote_copy(
            src_ref=full.at[chunk(mx)], dst_ref=full.at[chunk(mx)],
            send_sem=s4.at[d - 1], recv_sem=r4.at[d - 1],
            device_id=(along_x(d), my), device_id_type=MESH)
        for d in range(1, nx)
    ]))


def add_up_scratch(nx, ny, height):
    dma = pltpu.SemaphoreType.DMA
    rows = height // nx
    return [
        pltpu.VMEM((nx - 1, rows, 128), jnp.bfloat16),
        pltpu.VMEM((rows, 128), jnp.bfloat16),
        pltpu.VMEM((ny - 1, rows // ny, 128), jnp.bfloat16),
        dma((nx - 1,)), dma((nx - 1,)), dma((ny - 1,)), dma((ny - 1,)),
        dma((ny - 1,)), dma((ny - 1,)), dma((nx - 1,)), dma((nx - 1,)),
    ]


AROUND = [(dx, dy) for dx in (-1, 0, 1) for dy in (-1, 0, 1) if (dx, dy) != (0, 0)]


def act(v, small):
    return 0.2 * v + 0.8 * (jnp.maximum(v, 0.0) + jnp.log(1.0 + small))


def slope(v, small):
    share = 1.0 / (1.0 + small)
    return 0.2 + 0.8 * jnp.where(v >= 0.0, share, small * share)


def leaving(step, size, width):
    return {1: pl.ds(size - width, width), -1: pl.ds(0, width), 0: pl.ds(0, size)}[step]


def landing(step, size, width):
    return {1: pl.ds(0, width), -1: pl.ds(width + size, width), 0: pl.ds(width, size)}[step]


def rim_copies(nx, ny, src, dst, width, send, recv, whole=False):
    mx, my = lax.axis_index("gx"), lax.axis_index("gy")
    copies = []
    for k, (dx, dy) in enumerate(AROUND):
        if whole:
            part, spot = src, dst.at[1 - dx, 1 - dy]
        else:
            part = src.at[leaving(dx, src.shape[0], width), leaving(dy, src.shape[1], width)]
            spot = dst.at[landing(dx, src.shape[0], width), landing(dy, src.shape[1], width)]
        copies.append(pltpu.make_async_remote_copy(
            src_ref=part, dst_ref=spot, send_sem=send.at[k], recv_sem=recv.at[k],
            device_id=(lax.rem(mx + dx + nx, nx), lax.rem(my + dy + ny, ny)), device_id_type=MESH))
    return copies


def shifted(cells):
    flat = cells.reshape((-1,) + cells.shape[-2:])
    depth = flat.shape[1]
    place = lax.broadcasted_iota(jnp.int32, flat.shape, 1)
    lower = jnp.where(place == 0, 0.0, pltpu.roll(flat, 1, 1))
    upper = jnp.where(place == depth - 1, 0.0, pltpu.roll(flat, depth - 1, 1))
    return lower.reshape(cells.shape), upper.reshape(cells.shape)


def coarse_taps(cells):
    cells = cells.astype(jnp.float32)
    lower, upper = shifted(cells)
    return jnp.concatenate([lower, cells, upper], axis=-1).astype(jnp.bfloat16)


def fine_taps(cells):
    lower, upper = shifted(cells)
    lane = lax.broadcasted_iota(jnp.int32, cells.shape, cells.ndim - 1)
    return jnp.where(lane < cells.shape[-1] // 2, upper, lower).astype(jnp.bfloat16)


def conv(taps, weights, start, rows, cols):
    total = None
    for k in range(9):
        ox, oy = start + k // 3, start + k % 3
        piece = taps[ox : ox + rows, oy : oy + cols]
        piece = piece.reshape(-1, piece.shape[-1])
        term = jnp.dot(piece, weights[k], preferred_element_type=jnp.float32)
        total = term if total is None else total + term
    return total.reshape(rows, cols, -1, weights.shape[2])


def spread_edge(values, axis, inner):
    first, mid, last = values
    shape = list(mid.shape)
    shape[axis] = inner
    return jnp.concatenate([first, jnp.broadcast_to(mid, shape), last], axis=axis)


def block_kernel(nx, ny, fine_scale, coarse_scale, field, cot, tile, w_first, w_first_t, b_first, w_upper, w_upper_t,
                 w_second, w_second_t, b_second, out_field, out_grad, out_sums,
                 field_ext, cot_ext, tile_ext, ctaps, ftaps, gtaps, rim_ext, rim_out, part, full,
                 first_in, line, line_in, s_f, r_f, s_c, r_c, s_t, r_t, s_g, r_g, *sems):
    mx, my = lax.axis_index("gx"), lax.axis_index("gy")
    rows, cols, depth, chans = field.shape
    fr, fc = 2 * rows, 2 * cols
    barrier = pltpu.get_barrier_semaphore()
    peers = {((dx + nx) % nx, (dy + ny) % ny) for dx, dy in AROUND}
    peers |= {(d, 0) for d in range(1, nx)} | {(0, d) for d in range(1, ny)}
    for dx, dy in sorted(peers):
        pl.semaphore_signal(barrier, inc=1, device_id=(lax.rem(mx + dx, nx), lax.rem(my + dy, ny)), device_id_type=MESH)
    pl.semaphore_wait(barrier, len(peers))
    field_copies = rim_copies(nx, ny, field, field_ext, 2, s_f, r_f)
    cot_copies = rim_copies(nx, ny, cot, cot_ext, 1, s_c, r_c)
    tile_copies = rim_copies(nx, ny, tile, tile_ext, 1, s_t, r_t, True)
    for copy in field_copies + cot_copies + tile_copies:
        copy.start()
    field_ext[2 : 2 + rows, 2 : 2 + cols] = field[...]
    cot_ext[1 : 1 + fr, 1 : 1 + fc] = cot[...]
    tile_ext[1, 1] = tile[...]
    for copy in field_copies:
        copy.wait()

    ctaps[...] = coarse_taps(field_ext[...])
    pre_first = conv(ctaps, w_first, 0, rows + 2, cols + 2) + b_first[...]
    small = jnp.exp(-jnp.abs(pre_first))
    hidden = act(pre_first, small).astype(jnp.bfloat16)
    slope_first = slope(pre_first, small)[1 : 1 + rows, 1 : 1 + cols]
    upper = jnp.dot(hidden.reshape(-1, chans), w_upper[...], preferred_element_type=jnp.float32)
    upper = upper.reshape(rows + 2, cols + 2, depth, 8 * chans)
    wide = 2 * chans
    sides = []
    for a in (0, 1):
        pair = [upper[..., (2 * a + b) * wide : (2 * a + b + 1) * wide] for b in (0, 1)]
        sides.append(jnp.stack(pair, axis=2).reshape(rows + 2, fc + 4, depth, wide))
    upper = jnp.stack(sides, axis=1).reshape(fr + 4, fc + 4, depth, wide)
    ftaps[..., :wide] = upper.astype(jnp.bfloat16)
    ftaps[..., wide:] = fine_taps(ftaps[..., :wide].astype(jnp.float32))

    pre_second = conv(ftaps, w_second, 0, fr + 2, fc + 2) + b_second[...]
    small = jnp.exp(-jnp.abs(pre_second))
    out_field[...] = act(pre_second, small)[1 : 1 + fr, 1 : 1 + fc].astype(jnp.bfloat16)
    for copy in cot_copies + tile_copies:
        copy.wait()
    tiles = tile_ext[...].astype(jnp.float32)
    bands = [spread_edge([tiles[i, j][None] for j in range(3)], 0, fc)[None] for i in range(3)]
    weight = spread_edge(bands, 0, fr)
    grad_pre = weight * cot_ext[...].astype(jnp.float32) * slope(pre_second, small)
    gtaps[..., :wide] = grad_pre.astype(jnp.bfloat16)
    gtaps[..., wide:] = fine_taps(gtaps[..., :wide].astype(jnp.float32))

    grad_up = conv(gtaps, w_second_t, 0, fr, fc).astype(jnp.bfloat16)
    six = grad_up.reshape(rows, 2, cols, 2, depth, wide)
    corner = {(a, b): six[:, a, :, b].reshape(-1, wide) for a in (0, 1) for b in (0, 1)}
    grad_hidden = sum(
        jnp.dot(corner[a, b], w_upper_t[2 * a + b], preferred_element_type=jnp.float32)
        for a in (0, 1) for b in (0, 1)
    )
    grad_first = (grad_hidden.reshape(rows, cols, depth, chans) * slope_first).astype(jnp.bfloat16)
    rim_out[...] = grad_first
    rim_ext[1 : 1 + rows, 1 : 1 + cols] = grad_first
    rim = rim_copies(nx, ny, rim_out, rim_ext, 1, s_g, r_g)
    for copy in rim:
        copy.start()

    part[31 * chans :, :] = jnp.zeros((part.shape[0] - 31 * chans, 128), jnp.bfloat16)
    own_hidden = hidden[1 : 1 + rows, 1 : 1 + cols].reshape(-1, chans)
    hidden_t = own_hidden.astype(jnp.float32).T.astype(jnp.bfloat16)
    for a in (0, 1):
        for b in (0, 1):
            at = (27 + 2 * a + b) * chans
            term = jnp.dot(hidden_t, corner[a, b], preferred_element_type=jnp.float32)
            part[at : at + chans, :] = (term * coarse_scale).astype(jnp.bfloat16)
    own_grad = gtaps[1 : 1 + fr, 1 : 1 + fc, :, :wide].reshape(-1, wide)
    own_grad_t = own_grad.astype(jnp.float32).T.astype(jnp.bfloat16)
    first_t = grad_first.reshape(-1, chans).astype(jnp.float32).T.astype(jnp.bfloat16)
    for k in range(9):
        ox, oy = k // 3, k % 3
        piece = ftaps[1 + ox : 1 + ox + fr, 1 + oy : 1 + oy + fc].reshape(-1, 2 * wide)
        two = jnp.dot(own_grad_t, piece, preferred_element_type=jnp.float32) * fine_scale
        even, odd = two[:chans], two[chans:]
        tap0 = odd[:, :chans] + even[:, 3 * chans :]
        tap1 = even[:, :chans] + odd[:, chans : 2 * chans]
        tap2 = even[:, chans : 2 * chans] + odd[:, 2 * chans : 3 * chans]
        piece = ctaps[1 + ox : 1 + ox + rows, 1 + oy : 1 + oy + cols].reshape(-1, 3 * chans)
        one = jnp.dot(first_t, piece, preferred_element_type=jnp.float32) * coarse_scale
        at = 3 * k * chans
        part[at : at + chans, :] = jnp.concatenate([tap0, tap1], axis=1).astype(jnp.bfloat16)
        part[at + chans : at + 2 * chans, :] = one[:, :wide].astype(jnp.bfloat16)
        part[at + 2 * chans : at + 3 * chans, :] = jnp.concatenate([tap2, one[:, wide:]], axis=1).astype(jnp.bfloat16)

    for copy in rim:
        copy.wait()
    grad_in = conv(coarse_taps(rim_ext[...]), w_first_t, 0, rows, cols)
    out_grad[...] = grad_in.astype(jnp.bfloat16)
    add_up(nx, ny, part, full, first_in, line, line_in, sems)
    out_sums[...] = full[...].astype(jnp.float32)


def flip_taps(weights):
    return jnp.transpose(weights[::-1], (0, 2, 1))


def pair_taps(weights):
    w = weights.reshape(9, 3, weights.shape[1], weights.shape[2])
    none = jnp.zeros_like(w[:, 0])
    even = jnp.concatenate([w[:, 1], w[:, 2], none, w[:, 0]], axis=1)
    odd = jnp.concatenate([w[:, 0], w[:, 1], w[:, 2], none], axis=1)
    return jnp.concatenate([even, odd], axis=2)


def per_device(field_in, w_first, b_first, w_upper, w_second, b_second, cotangent, tile_weights):
    rows, cols, flat = field_in.shape
    chans = w_first.shape[1]
    depth = flat // chans
    wide = 2 * chans
    nx, ny = lax.axis_size("gx"), lax.axis_size("gy")
    coarse_scale = 1.0 / math.sqrt(rows * cols * depth * nx * ny)
    fine_scale = 1.0 / math.sqrt(8 * rows * cols * depth * nx * ny)
    fr, fc = 2 * rows, 2 * cols
    unit = 16 * nx * ny
    height = -(-31 * chans // unit) * unit
    bf, dma = jnp.bfloat16, pltpu.SemaphoreType.DMA
    tile = jnp.broadcast_to(tile_weights.astype(bf), (16, wide))
    up = w_upper.reshape(4, 2, chans, chans)
    args = (
        field_in.reshape(rows, cols, depth, chans),
        cotangent.reshape(fr, fc, depth, wide),
        tile,
        w_first.reshape(9, 3 * chans, chans),
        flip_taps(w_first).reshape(9, 3 * chans, chans),
        b_first.reshape(1, chans),
        jnp.transpose(w_upper, (1, 0, 2)).reshape(chans, 8 * chans),
        jnp.transpose(up, (0, 1, 3, 2)).reshape(4, wide, chans),
        pair_taps(w_second),
        pair_taps(flip_taps(w_second)),
        jnp.concatenate([b_second, b_second]).reshape(1, wide),
    )
    vmem = pl.BlockSpec(memory_space=pltpu.VMEM)
    out, grad, sums = pl.pallas_call(
        functools.partial(block_kernel, nx, ny, fine_scale, coarse_scale),
        out_shape=(
            jax.ShapeDtypeStruct((fr, fc, depth, wide), bf),
            jax.ShapeDtypeStruct((rows, cols, depth, chans), bf),
            jax.ShapeDtypeStruct((height, 128), jnp.float32),
        ),
        in_specs=[vmem] * len(args),
        out_specs=(vmem, vmem, vmem),
        scratch_shapes=[
            pltpu.VMEM((rows + 4, cols + 4, depth, chans), bf),
            pltpu.VMEM((fr + 2, fc + 2, depth, wide), bf),
            pltpu.VMEM((3, 3, 16, wide), bf),
            pltpu.VMEM((rows + 4, cols + 4, depth, 3 * chans), bf),
            pltpu.VMEM((fr + 4, fc + 4, depth, 2 * wide), bf),
            pltpu.VMEM((fr + 2, fc + 2, depth, 2 * wide), bf),
            pltpu.VMEM((rows + 2, cols + 2, depth, chans), bf),
            pltpu.VMEM((rows, cols, depth, chans), bf),
            pltpu.VMEM((height, 128), bf),
            pltpu.VMEM((height, 128), bf),
        ] + add_up_scratch(nx, ny, height)[:3] + [dma((8,))] * 8 + add_up_scratch(nx, ny, height)[3:],
        compiler_params=pltpu.CompilerParams(collective_id=0, has_side_effects=True, vmem_limit_bytes=48 << 20),
    )(*args)
    taps = sums[: 27 * chans].reshape(9, 3, chans, 2, chans)
    second = jnp.stack([taps[:, 0, :, 0], taps[:, 0, :, 1], taps[:, 2, :, 0]], axis=1)
    first = jnp.stack([taps[:, 1, :, 0], taps[:, 1, :, 1], taps[:, 2, :, 1]], axis=1)
    upper = sums[27 * chans : 31 * chans].reshape(4, chans, 2, chans)
    return (
        out.reshape(fr, fc, 2 * flat),
        grad.reshape(rows, cols, flat),
        jnp.transpose(first.reshape(27, chans, chans), (0, 2, 1)),
        jnp.transpose(upper, (0, 2, 1, 3)).reshape(8, chans, chans),
        jnp.transpose(second.reshape(27, chans, chans), (0, 2, 1)),
    )


def solution(mesh):
    in_specs = (P("gx", "gy", None), P(), P(), P(), P(), P(), P("gx", "gy", None), P("gx", "gy"))
    out_specs = (P("gx", "gy", None), P("gx", "gy", None), P(), P(), P())
    return jax.shard_map(
        per_device, mesh=mesh, in_specs=in_specs, out_specs=out_specs, check_vma=False
    )
```

time: 134 us -> 61.8 us (0.46)
  matrix products: 40.9 us -> 0 us
  starting transfers between devices: 26.3 us -> 0 us
  Pallas kernels: 22.9 us -> 46.4 us
  local copies, waits for them, and re-layouts: 27 us -> 11.9 us
  waiting for transfers between devices: 9.35 us -> 0 us
  other arithmetic: 4.9 us -> 1.55 us
    dot_general x165 -> x0, matrix products: 40.9 us -> none  [the longest x108 26.5 us: conv_local(): jnp.dot(piece, weights[k], preferred_element_type=jnp.float32)]
    ppermute x16 -> x0, starting transfers between devices: 26.3 us -> none  [the longest x8 19.8 us: extended(): lax.ppermute(head, axis, [((i + 1) % count, i) for i in range(count)])]
    pallas_call x1, Pallas kernels: 22.9 us -> 46.4 us  [per_device(): pl.pallas_call(functools.partial(block_kernel, nx, ny, fine_scale, coarse...]
    slice x23 -> x3, local copies, waits for them, and re-layouts: 12.1 us -> 1.29 us  [the longest x1 1.23 us: per_device(): taps[:, 0, :, 0]]
    ppermute x16 -> x0, waiting for transfers between devices: 9.35 us -> none  [the longest x8 6.3 us: extended(): lax.ppermute(tail, axis, [(i, (i + 1) % count) for i in range(count)])]
    convert_element_type x2 -> x0, other arithmetic: 3.75 us -> none  [per_device(): grad_pre = (weight_grid * fine_cot * slope_fine).reshape(2 * rows, 2 * co...]
    another operation x0 -> x3, local copies, waits for them, and re-layouts: none -> 2.46 us  [the longest x1 1.22 us: per_device(): jnp.stack([taps[:, 1, :, 0], taps[:, 1, :, 1], taps[:, 2, :, 1]], axis=1)]
    mul x5 -> x0, local copies, waits for them, and re-layouts: 2.1 us -> none  [the longest x1 1.42 us: per_device(): weight_grid * fine_cot * slope_fine]
  transfers between devices with their start and end apart: 16 -> 0, of which waited for: 9 -> 0; matrix products, arithmetic and copies ran while one was open for 15% -> 0% of each run, Pallas kernels for 17% -> 0%
where the time goes in v2:
time: 61.8 us; the launch traced here: 61.4 us
  Pallas kernels  46.4 us (75%)
  local copies, waits for them, and re-layouts  11.9 us (19%)
  other arithmetic  1.55 us (3%)
  between operations  1.51 us (2%)
    pallas_call x1, Pallas kernels, per_device(): pl.pallas_call(functools.partial(block_kernel, nx, ny, fine_scale, coarse...  46.4 us
    unnamed x8, local copies, waits for them, and re-layouts  1.32 us

profile of v2, /device:TPU:0, one launch (start us, length us, event | category | flops | bytes accessed | tf_op | source)
XLA Modules:
  0.0 61.4 jit_solution(3231353620387744224)
XLA Ops:
  0.6 0.0 copy-start
  1.3 0.8 %maximum_bitcast_fusion.b_second = f32[1,128]{1,0:T(1,128)S(1)} fusion(f32[64]{0:T(128)} %param.13), kind=kLoop, calls=%fused_computation.18 | loop fusion | flops 128 | bytes 768 | tf_op jit(solution)/shard_map/reshape | solution.py:304
  2.2 0.9 %reshape.64.field = bf16[4,4,16,64]{3,2,1,0:T(8,128)(2,1)S(1)} reshape(bf16[4,4,1024]{2,1,0:T(4,128)(2,1)} %param.8) | data formatting | bytes 65536 | tf_op jit(solution)/shard_map/reshape | solution.py:294
  3.0 1.0 %copy.24 = bf16[64,8,64]{2,1,0:T(8,128)(2,1)S(1)} copy(bf16[64,8,64]{2,0,1:T(8,128)(2,1)} %bitcast.88) | data formatting | bytes 131072 | tf_op jit(solution)/shard_map/transpose | solution.py:300
  4.0 0.1 reshape.69.w_upper
  4.2 1.0 %copy.25 = bf16[4,2,64,64]{2,3,1,0:T(8,128)(2,1)S(1)} copy(bf16[4,2,64,64]{3,2,1,0:T(8,128)(2,1)} %bitcast.89) | data formatting | bytes 131072 | tf_op jit(solution)/shard_map/reshape | solution.py:292
  5.2 0.0 copy-start.2
  5.2 1.0 %copy.52 = bf16[8,8,16,128]{3,2,1,0:T(8,128)(2,1)S(1)} copy(bf16[8,8,16,128]{3,1,2,0:T(8,128)(2,1)} %bitcast.90) | data formatting | bytes 524288
  6.3 0.0 copy-done
  6.3 0.2 copy.23
  6.6 0.0 copy-done.2
  6.6 0.2 copy.29
  6.9 0.1 slice_bitcast_fusion
  6.9 0.0 copy-start.1
  7.0 0.6 fusion.3
  7.6 0.0 copy-done.1
  7.6 46.4 %shard_map.119 = (bf16[8,8,16,128]{3,2,1,0:T(8,128)(2,1)S(1)}, bf16[4,4,16,64]{3,2,1,0:T(8,128)(2,1)S(1)}, f32[2048,128]{1,0:T(8,128)S(1)}) custom-call(bf16[4,4,16,64]{3,2,1,0:T(8,128)(2,1)S(1)} %reshape.64.field, bf16[8,8,16,128]{3,2,1,0:T(8,128)(2,1)S(1)} %copy.52, bf16[16,128]{1,0:T(8,128)(2,1)S(1)} %broadcast_in_dim.8.tile, ...), custom_call_target="tpu_custom_call" | custom-call | tf_op jit(solution)/shard_map/pallas_call | solution.py:307
  54.0 0.8 %reshape.75 = bf16[8,8,2048]{2,1,0:T(8,128)(2,1)} reshape(bf16[8,8,16,128]{3,2,1,0:T(8,128)(2,1)S(1)} %get-tuple-element.8) | data formatting | bytes 524288 | tf_op jit(solution)/shard_map/reshape | solution.py:335
  54.9 0.7 %reshape.76 = bf16[4,4,1024]{2,1,0:T(4,128)(2,1)} reshape(bf16[4,4,16,64]{3,2,1,0:T(8,128)(2,1)S(1)} %get-tuple-element.9) | data formatting | bytes 65536 | tf_op jit(solution)/shard_map/reshape | solution.py:336
  55.6 0.1 slice.54
  55.7 0.2 reshape.79
  55.9 0.7 %copy.36 = f32[4,2,64,64]{3,2,1,0:T(8,128)} copy(f32[4,2,64,64]{3,1,2,0:T(2,128)S(1)} %bitcast.85) | data formatting | bytes 262144 | tf_op jit(solution)/shard_map/transpose | solution.py:338
  56.6 1.0 %reshape.77 = f32[9,3,64,2,64]{4,3,2,1,0:T(2,128)S(1)} reshape(f32[1728,128]{1,0:T(8,128)S(1)} %slice.54) | data formatting | bytes 1769472 | tf_op jit(solution)/shard_map/reshape | solution.py:330
  57.6 1.2 %fusion.4 = (f32[9,1,64,1,64]{4,3,2,1,0:T(1,128)S(1)}, f32[9,1,64,1,64]{4,3,2,1,0:T(1,128)S(1)}, f32[9,1,64,1,64]{4,3,2,1,0:T(1,128)S(1)}, f32[9,1,64,1,64]{4,3,...) fusion(f32[9,3,64,2,64]{4,3,2,1,0:T(2,128)S(1)} %reshape.77), kind=kLoop, calls=%fused_computation.19 | loop fusion | bytes 1769472 | tf_op jit(solution)/shard_map/slice | solution.py:331
  58.8 0.1 pad_maximum_fusion.1
  58.9 1.2 %copy.39 = f32[9,3,64,64]{2,3,1,0:T(8,128)} copy(f32[9,3,64,64]{3,2,0,1:T(8,128)S(1)} %pad_maximum_fusion.1) | data formatting | bytes 884736 | tf_op jit(solution)/shard_map/stack | solution.py:331
  60.1 0.1 pad_maximum_fusion
  60.2 1.2 %copy.35 = f32[9,3,64,64]{2,3,1,0:T(8,128)} copy(f32[9,3,64,64]{3,2,0,1:T(8,128)S(1)} %pad_maximum_fusion) | data formatting | bytes 884736 | tf_op jit(solution)/shard_map/stack | solution.py:332
  (5 shorter events, 0.1 us)
Async XLA Ops:
  0.6 5.6 %copy-start = (bf16[27,64,64]{2,1,0:T(8,128)(2,1)S(1)}, bf16[27,64,64]{2,1,0:T(8,128)(2,1)}, u32[]{:S(2)}) copy-start(bf16[27,64,64]{2,1,0:T(8,128)(2,1)} %param.9) | copy-start | bytes 663556
  5.2 1.4 %copy-start.2 = (bf16[27,64,64]{2,1,0:T(8,128)(2,1)S(1)}, bf16[27,64,64]{2,1,0:T(8,128)(2,1)}, u32[]{:S(2)}) copy-start(bf16[27,64,64]{2,1,0:T(8,128)(2,1)} %param.12) | copy-start | bytes 663556
  6.9 0.7 %copy-start.1 = (f32[64]{0:T(128)S(1)}, f32[64]{0:T(128)}, u32[]{:S(2)}) copy-start(f32[64]{0:T(128)} %param.10) | copy-start | bytes 772

commit v3 on v2

v3 whole, which is shorter than its diff:
```python
import functools
import math

import jax
import jax.numpy as jnp
from jax import lax
from jax.experimental import pallas as pl
from jax.experimental.pallas import tpu as pltpu
from jax.sharding import PartitionSpec as P


MESH = pl.DeviceIdType.MESH


def add_up(nx, ny, used, part, full, first_in, line, line_in, sems):
    mx, my = lax.axis_index("gx"), lax.axis_index("gy")
    small = part.shape[1] // ny
    s1, r1, s2, r2, s3, r3, s4, r4 = sems

    def piece(i):
        return pl.ds(pl.multiple_of(i * small, 16), small)

    def along_x(d):
        return lax.rem(mx + d, nx)

    def along_y(d):
        return lax.rem(my + d, ny)

    def over_x(pair, send, recv):
        copies = [
            pltpu.make_async_remote_copy(
                src_ref=pair(d)[0], dst_ref=pair(d)[1], send_sem=send.at[d - 1], recv_sem=recv.at[d - 1],
                device_id=(along_x(d), my), device_id_type=MESH)
            for d in range(1, nx)
        ]
        for copy in copies:
            copy.start()
        return copies

    def over_y(pair, send, recv):
        copies = [
            pltpu.make_async_remote_copy(
                src_ref=pair(d)[0], dst_ref=pair(d)[1], send_sem=send.at[d - 1], recv_sem=recv.at[d - 1],
                device_id=(mx, along_y(d)), device_id_type=MESH)
            for d in range(1, ny)
        ]
        for copy in copies:
            copy.start()
        return copies

    copies = over_x(lambda d: (part.at[along_x(d), pl.ds(0, used)], first_in.at[d - 1]), s1, r1)
    yield
    for copy in copies:
        copy.wait()
    total = part[mx, :used, :].astype(jnp.float32)
    for d in range(nx - 1):
        total += first_in[d].astype(jnp.float32)
    line[:used, :] = total.astype(jnp.bfloat16)
    if used < line.shape[0]:
        line[used:, :] = jnp.zeros((line.shape[0] - used, 128), jnp.bfloat16)
    copies = over_y(lambda d: (line.at[piece(along_y(d))], line_in.at[d - 1]), s2, r2)
    yield
    for copy in copies:
        copy.wait()
    total = line[piece(my), :].astype(jnp.float32)
    for d in range(ny - 1):
        total += line_in[d].astype(jnp.float32)
    full[mx, piece(my), :] = total.astype(jnp.bfloat16)
    copies = over_y(lambda d: (full.at[mx, piece(my)], full.at[mx, piece(my)]), s3, r3)
    yield
    for copy in copies:
        copy.wait()
    whole = pl.ds(0, used)
    copies = over_x(lambda d: (full.at[mx, whole], full.at[mx, whole]), s4, r4)
    yield
    for copy in copies:
        copy.wait()


def sum_sizes(nx, ny, blocks, chans):
    used = -(-blocks * chans // (16 * nx)) * 16
    return used, -(-used // (16 * ny)) * 16 * ny


def add_up_scratch(nx, ny, blocks, chans):
    used, chunk = sum_sizes(nx, ny, blocks, chans)
    bf, dma = jnp.bfloat16, pltpu.SemaphoreType.DMA
    return [
        pltpu.VMEM((nx, chunk, 128), bf),
        pltpu.VMEM((nx, chunk, 128), bf),
        pltpu.VMEM((nx - 1, used, 128), bf),
        pltpu.VMEM((chunk, 128), bf),
        pltpu.VMEM((ny - 1, chunk // ny, 128), bf),
        dma((nx - 1,)), dma((nx - 1,)), dma((ny - 1,)), dma((ny - 1,)),
        dma((ny - 1,)), dma((ny - 1,)), dma((nx - 1,)), dma((nx - 1,)),
    ]


def segments(used, start, stop):
    found = []
    while start < stop:
        chunk, row = start // used, start % used
        size = min(used - row, stop - start)
        found.append((chunk, row, size))
        start += size
    return found


def put_block(part, used, block, value):
    at, value = 0, value.astype(jnp.bfloat16)
    height = value.shape[0]
    for chunk, row, size in segments(used, block * height, (block + 1) * height):
        part[chunk, row : row + size, :] = value[at : at + size]
        at += size


def put_taps(part, used, terms):
    wide = part.shape[2]
    for k in range(9):
        put_block(part, used, k, terms[k][:, :wide])
    for j in range(5):
        left = terms[2 * j][:, wide:]
        right = terms[2 * j + 1][:, wide:] if 2 * j + 1 < 9 else jnp.zeros_like(left)
        put_block(part, used, 9 + j, jnp.concatenate([left, right], axis=1))


def clear_end(part, used, rows):
    for chunk, row, size in segments(used, rows, part.shape[0] * used):
        part[chunk, row : row + size, :] = jnp.zeros((size, part.shape[2]), jnp.bfloat16)


def get_block(full, used, block, height):
    pieces = [full[c, r : r + n, :] for c, r, n in segments(used, block * height, (block + 1) * height)]
    return jnp.concatenate(pieces, axis=0).astype(jnp.float32) if len(pieces) > 1 else pieces[0].astype(jnp.float32)


def get_taps(full, used, out):
    chans = out.shape[1]
    for k in range(9):
        out[3 * k : 3 * k + 2] = get_block(full, used, k, chans).T.reshape(2, chans, chans)
    for j in range(5):
        both = get_block(full, used, 9 + j, chans).T
        out[6 * j + 2] = both[:chans]
        if 2 * j + 1 < 9:
            out[6 * j + 5] = both[chans:]


AROUND = [(dx, dy) for dx in (-1, 0, 1) for dy in (-1, 0, 1) if (dx, dy) != (0, 0)]


def act(v, small):
    return 0.2 * v + 0.8 * (jnp.maximum(v, 0.0) + jnp.log(1.0 + small))


def slope(v, small):
    share = 1.0 / (1.0 + small)
    return 0.2 + 0.8 * jnp.where(v >= 0.0, share, small * share)


def leaving(step, size, width):
    return {1: pl.ds(size - width, width), -1: pl.ds(0, width), 0: pl.ds(0, size)}[step]


def landing(step, size, width):
    return {1: pl.ds(0, width), -1: pl.ds(width + size, width), 0: pl.ds(width, size)}[step]


def rim_copies(nx, ny, src, dst, width, send, recv, whole=False):
    mx, my = lax.axis_index("gx"), lax.axis_index("gy")
    copies = []
    for k, (dx, dy) in enumerate(AROUND):
        if whole:
            part, spot = src, dst.at[1 - dx, 1 - dy]
        else:
            part = src.at[leaving(dx, src.shape[0], width), leaving(dy, src.shape[1], width)]
            spot = dst.at[landing(dx, src.shape[0], width), landing(dy, src.shape[1], width)]
        copies.append(pltpu.make_async_remote_copy(
            src_ref=part, dst_ref=spot, send_sem=send.at[k], recv_sem=recv.at[k],
            device_id=(lax.rem(mx + dx + nx, nx), lax.rem(my + dy + ny, ny)), device_id_type=MESH))
    return copies


def shifted(cells):
    flat = cells.reshape((-1,) + cells.shape[-2:])
    depth = flat.shape[1]
    place = lax.broadcasted_iota(jnp.int32, flat.shape, 1)
    lower = jnp.where(place == 0, 0.0, pltpu.roll(flat, 1, 1))
    upper = jnp.where(place == depth - 1, 0.0, pltpu.roll(flat, depth - 1, 1))
    return lower.reshape(cells.shape), upper.reshape(cells.shape)


def coarse_taps(cells):
    cells = cells.astype(jnp.float32)
    lower, upper = shifted(cells)
    return jnp.concatenate([lower, cells, upper], axis=-1).astype(jnp.bfloat16)


def fine_taps(cells):
    lower, upper = shifted(cells)
    lane = lax.broadcasted_iota(jnp.int32, cells.shape, cells.ndim - 1)
    return jnp.where(lane < cells.shape[-1] // 2, upper, lower).astype(jnp.bfloat16)


def times(left, right):
    return jnp.dot(left, right, preferred_element_type=jnp.float32)


def times_t(left, right):
    return lax.dot_general(left, right, (((1,), (1,)), ((), ())), preferred_element_type=jnp.float32)


def conv(taps, weights, rows, cols, product=times):
    total = None
    for k in range(9):
        ox, oy = k // 3, k % 3
        piece = taps[ox : ox + rows, oy : oy + cols]
        piece = piece.reshape(-1, piece.shape[-1])
        term = product(piece, weights[k])
        total = term if total is None else total + term
    return total.reshape(rows, cols, -1, total.shape[1])


def spread_edge(values, axis, inner):
    first, mid, last = values
    shape = list(mid.shape)
    shape[axis] = inner
    return jnp.concatenate([first, jnp.broadcast_to(mid, shape), last], axis=axis)


def block_kernel(nx, ny, fine_scale, coarse_scale, field, cot, tile, w_first, b_first, w_upper, w_second, b_second,
                 out_field, out_grad, out_first, out_upper, out_second,
                 field_ext, cot_ext, tile_ext, ctaps, ftaps, gtaps, rim_ext, rim_out,
                 first_t, up_row, second_n, second_t, s_f, r_f, s_c, r_c, s_t, r_t, s_g, r_g, *groups):
    mx, my = lax.axis_index("gx"), lax.axis_index("gy")
    rows, cols, depth, chans = field.shape
    fr, fc = 2 * rows, 2 * cols
    wide = 2 * chans
    part_a, full_a, *rest_a = groups[: len(groups) // 2]
    part_b, full_b, *rest_b = groups[len(groups) // 2 :]
    used_a, used_b = rest_a[0].shape[1], rest_b[0].shape[1]
    barrier = pltpu.get_barrier_semaphore()
    peers = {((dx + nx) % nx, (dy + ny) % ny) for dx, dy in AROUND}
    peers |= {(d, 0) for d in range(1, nx)} | {(0, d) for d in range(1, ny)}
    for dx, dy in sorted(peers):
        pl.semaphore_signal(barrier, inc=1, device_id=(lax.rem(mx + dx, nx), lax.rem(my + dy, ny)), device_id_type=MESH)
    pl.semaphore_wait(barrier, len(peers))
    field_copies = rim_copies(nx, ny, field, field_ext, 2, s_f, r_f)
    cot_copies = rim_copies(nx, ny, cot, cot_ext, 1, s_c, r_c)
    tile_copies = rim_copies(nx, ny, tile, tile_ext, 1, s_t, r_t, True)
    for copy in field_copies + cot_copies + tile_copies:
        copy.start()
    field_ext[2 : 2 + rows, 2 : 2 + cols] = field[...]
    cot_ext[1 : 1 + fr, 1 : 1 + fc] = cot[...]
    tile_ext[1, 1] = tile[...]
    none = jnp.zeros((chans, chans), jnp.bfloat16)
    for k in range(9):
        low, mid, high = w_second[3 * k], w_second[3 * k + 1], w_second[3 * k + 2]
        second_n[k, :chans] = jnp.concatenate([mid, low], axis=1)
        second_n[k, chans : 2 * chans] = jnp.concatenate([high, mid], axis=1)
        second_n[k, 2 * chans : 3 * chans] = jnp.concatenate([none, high], axis=1)
        second_n[k, 3 * chans :] = jnp.concatenate([low, none], axis=1)
        second_t[8 - k, :chans] = jnp.concatenate([mid, low, none, high], axis=1)
        second_t[8 - k, chans:] = jnp.concatenate([high, mid, low, none], axis=1)
        first_t[8 - k] = jnp.concatenate([w_first[3 * k + 2], w_first[3 * k + 1], w_first[3 * k]], axis=1)
    up_row[...] = jnp.concatenate([w_upper[k] for k in range(8)], axis=1)
    for copy in field_copies:
        copy.wait()

    ctaps[...] = coarse_taps(field_ext[...])
    pre_first = conv(ctaps, w_first[...].reshape(9, 3 * chans, chans), rows + 2, cols + 2) + b_first[...]
    small = jnp.exp(-jnp.abs(pre_first))
    hidden = act(pre_first, small).astype(jnp.bfloat16)
    slope_first = slope(pre_first, small)[1 : 1 + rows, 1 : 1 + cols]
    upper = times(hidden.reshape(-1, chans), up_row[...])
    upper = upper.reshape(rows + 2, cols + 2, depth, 8 * chans)
    sides = []
    for a in (0, 1):
        pair = [upper[..., (2 * a + b) * wide : (2 * a + b + 1) * wide] for b in (0, 1)]
        sides.append(jnp.stack(pair, axis=2).reshape(rows + 2, fc + 4, depth, wide))
    upper = jnp.stack(sides, axis=1).reshape(fr + 4, fc + 4, depth, wide)
    ftaps[..., :wide] = upper.astype(jnp.bfloat16)
    ftaps[..., wide:] = fine_taps(ftaps[..., :wide].astype(jnp.float32))

    pre_second = conv(ftaps, second_n, fr + 2, fc + 2) + b_second[...]
    small = jnp.exp(-jnp.abs(pre_second))
    out_field[...] = act(pre_second, small)[1 : 1 + fr, 1 : 1 + fc].astype(jnp.bfloat16)
    for copy in cot_copies + tile_copies:
        copy.wait()
    tiles = tile_ext[...].astype(jnp.float32)
    bands = [spread_edge([tiles[i, j][None] for j in range(3)], 0, fc)[None] for i in range(3)]
    weight = spread_edge(bands, 0, fr)
    grad_pre = weight * cot_ext[...].astype(jnp.float32) * slope(pre_second, small)
    gtaps[..., :wide] = grad_pre.astype(jnp.bfloat16)
    gtaps[..., wide:] = fine_taps(gtaps[..., :wide].astype(jnp.float32))

    own_grad = gtaps[1 : 1 + fr, 1 : 1 + fc, :, :wide].reshape(-1, wide)
    own_grad_t = own_grad.astype(jnp.float32).T.astype(jnp.bfloat16)
    terms = []
    for k in range(9):
        ox, oy = 1 + k // 3, 1 + k % 3
        piece = ftaps[ox : ox + fr, oy : oy + fc].reshape(-1, 2 * wide)
        two = times(own_grad_t, piece) * fine_scale
        even, odd = two[:chans], two[chans:]
        tap0 = odd[:, :chans] + even[:, 3 * chans :]
        tap1 = even[:, :chans] + odd[:, chans : 2 * chans]
        tap2 = even[:, chans : 2 * chans] + odd[:, 2 * chans : 3 * chans]
        terms.append(jnp.concatenate([tap0, tap1, tap2], axis=1))
    put_taps(part_a, used_a, terms)
    clear_end(part_a, used_a, 14 * chans)
    sum_a = add_up(nx, ny, used_a, part_a, full_a, *rest_a[:3], rest_a[3:])
    next(sum_a)

    grad_up = conv(gtaps, second_t, fr, fc, times_t).astype(jnp.bfloat16)
    six = grad_up.reshape(rows, 2, cols, 2, depth, wide)
    corner = [six[:, a, :, b].reshape(-1, wide) for a in (0, 1) for b in (0, 1)]
    grad_hidden = times_t(jnp.concatenate(corner, axis=1), up_row[...])
    grad_first = (grad_hidden.reshape(rows, cols, depth, chans) * slope_first).astype(jnp.bfloat16)
    rim_out[...] = grad_first
    rim_ext[1 : 1 + rows, 1 : 1 + cols] = grad_first
    rim = rim_copies(nx, ny, rim_out, rim_ext, 1, s_g, r_g)
    for copy in rim:
        copy.start()
    next(sum_a)

    own_hidden = hidden[1 : 1 + rows, 1 : 1 + cols].reshape(-1, chans)
    hidden_t = own_hidden.astype(jnp.float32).T.astype(jnp.bfloat16)
    for k in range(4):
        put_block(part_b, used_b, 14 + k, times(hidden_t, corner[k]) * coarse_scale)
    grad_first_t = grad_first.reshape(-1, chans).astype(jnp.float32).T.astype(jnp.bfloat16)
    terms = []
    for k in range(9):
        ox, oy = 1 + k // 3, 1 + k % 3
        piece = ctaps[ox : ox + rows, oy : oy + cols].reshape(-1, 3 * chans)
        terms.append(times(grad_first_t, piece) * coarse_scale)
    put_taps(part_b, used_b, terms)
    clear_end(part_b, used_b, 18 * chans)
    sum_b = add_up(nx, ny, used_b, part_b, full_b, *rest_b[:3], rest_b[3:])
    next(sum_b)
    next(sum_a)
    for copy in rim:
        copy.wait()
    grad_in = conv(coarse_taps(rim_ext[...]), first_t, rows, cols, times_t)
    out_grad[...] = grad_in.astype(jnp.bfloat16)
    next(sum_a)
    next(sum_b)
    next(sum_b)
    next(sum_b)
    for _ in sum_a:
        pass
    get_taps(full_a, used_a, out_second)
    for _ in sum_b:
        pass
    get_taps(full_b, used_b, out_first)
    for k in range(4):
        both = get_block(full_b, used_b, 14 + k, chans)
        out_upper[2 * k] = both[:, :chans]
        out_upper[2 * k + 1] = both[:, chans:]


def per_device(field_in, w_first, b_first, w_upper, w_second, b_second, cotangent, tile_weights):
    rows, cols, flat = field_in.shape
    chans = w_first.shape[1]
    depth = flat // chans
    wide = 2 * chans
    nx, ny = lax.axis_size("gx"), lax.axis_size("gy")
    coarse_scale = 1.0 / math.sqrt(rows * cols * depth * nx * ny)
    fine_scale = 1.0 / math.sqrt(8 * rows * cols * depth * nx * ny)
    fr, fc = 2 * rows, 2 * cols
    bf, dma = jnp.bfloat16, pltpu.SemaphoreType.DMA
    args = (
        field_in.reshape(rows, cols, depth, chans),
        cotangent.reshape(fr, fc, depth, wide),
        jnp.broadcast_to(tile_weights.astype(bf), (16, wide)),
        w_first,
        b_first.reshape(1, chans),
        w_upper,
        w_second,
        jnp.concatenate([b_second, b_second]).reshape(1, wide),
    )
    vmem = pl.BlockSpec(memory_space=pltpu.VMEM)
    out, grad, first, upper, second = pl.pallas_call(
        functools.partial(block_kernel, nx, ny, fine_scale, coarse_scale),
        out_shape=(
            jax.ShapeDtypeStruct((fr, fc, depth, wide), bf),
            jax.ShapeDtypeStruct((rows, cols, depth, chans), bf),
            jax.ShapeDtypeStruct((27, chans, chans), jnp.float32),
            jax.ShapeDtypeStruct((8, chans, chans), jnp.float32),
            jax.ShapeDtypeStruct((27, chans, chans), jnp.float32),
        ),
        in_specs=[vmem] * len(args),
        out_specs=(vmem,) * 5,
        scratch_shapes=[
            pltpu.VMEM((rows + 4, cols + 4, depth, chans), bf),
            pltpu.VMEM((fr + 2, fc + 2, depth, wide), bf),
            pltpu.VMEM((3, 3, 16, wide), bf),
            pltpu.VMEM((rows + 4, cols + 4, depth, 3 * chans), bf),
            pltpu.VMEM((fr + 4, fc + 4, depth, 2 * wide), bf),
            pltpu.VMEM((fr + 2, fc + 2, depth, 2 * wide), bf),
            pltpu.VMEM((rows + 2, cols + 2, depth, chans), bf),
            pltpu.VMEM((rows, cols, depth, chans), bf),
            pltpu.VMEM((9, chans, 3 * chans), bf),
            pltpu.VMEM((chans, 8 * chans), bf),
            pltpu.VMEM((9, 2 * wide, wide), bf),
            pltpu.VMEM((9, wide, 2 * wide), bf),
        ] + [dma((8,))] * 8 + add_up_scratch(nx, ny, 14, chans) + add_up_scratch(nx, ny, 18, chans),
        compiler_params=pltpu.CompilerParams(collective_id=0, has_side_effects=True, vmem_limit_bytes=48 << 20),
    )(*args)
    return out.reshape(fr, fc, 2 * flat), grad.reshape(rows, cols, flat), first, upper, second


def solution(mesh):
    in_specs = (P("gx", "gy", None), P(), P(), P(), P(), P(), P("gx", "gy", None), P("gx", "gy"))
    out_specs = (P("gx", "gy", None), P("gx", "gy", None), P(), P(), P())
    return jax.shard_map(
        per_device, mesh=mesh, in_specs=in_specs, out_specs=out_specs, check_vma=False
    )
```

time: 61.8 us -> 51.6 us (0.83)
  Pallas kernels: 46.4 us -> 41.5 us
  local copies, waits for them, and re-layouts: 11.9 us -> 7.61 us
  other arithmetic: 1.55 us -> 0.81 us
    pallas_call x1, Pallas kernels: 46.4 us -> 41.5 us  [per_device(): pl.pallas_call(functools.partial(block_kernel, nx, ny, fine_scale, coarse...]
    unnamed x8 -> x12, local copies, waits for them, and re-layouts: 1.32 us -> 5.2 us
    another operation x3 -> x0, local copies, waits for them, and re-layouts: 2.46 us -> none  [the longest x1 1.22 us: per_device(): jnp.stack([taps[:, 1, :, 0], taps[:, 1, :, 1], taps[:, 2, :, 1]], axis=1)]
    reshape x4 -> x0, local copies, waits for them, and re-layouts: 2.34 us -> none  [the longest x1 1.02 us: per_device(): up = w_upper.reshape(4, 2, chans, chans)]
    transpose x4 -> x0, local copies, waits for them, and re-layouts: 1.99 us -> none  [the longest x1 1 us: per_device(): jnp.transpose(w_upper, (1, 0, 2)).reshape(chans, 8 * chans)]
    slice x3 -> x0, local copies, waits for them, and re-layouts: 1.29 us -> none  [the longest x1 1.23 us: per_device(): taps[:, 0, :, 0]]
where the time goes in v3:
time: 51.6 us; the launch traced here: 51.3 us
  Pallas kernels  41.5 us (80%)
  local copies, waits for them, and re-layouts  7.61 us (15%)
  between operations  1.4 us (3%)
  other arithmetic  0.81 us (2%)
    pallas_call x1, Pallas kernels, per_device(): pl.pallas_call(functools.partial(block_kernel, nx, ny, fine_scale, coarse...  41.5 us
    unnamed x12, local copies, waits for them, and re-layouts  5.2 us

profile of v3, /device:TPU:0, one launch (start us, length us, event | category | flops | bytes accessed | tf_op | source)
XLA Modules:
  0.0 51.3 jit_solution(537975020615612336)
XLA Ops:
  0.6 0.0 copy-start
  1.3 0.8 %maximum_bitcast_fusion.b_second = f32[1,128]{1,0:T(1,128)S(1)} fusion(f32[64]{0:T(128)} %param.13), kind=kLoop, calls=%fused_computation.1 | loop fusion | flops 128 | bytes 768 | tf_op jit(solution)/shard_map/reshape | solution.py:378
  2.2 0.9 %reshape.28.field = bf16[4,4,16,64]{3,2,1,0:T(8,128)(2,1)S(1)} reshape(bf16[4,4,1024]{2,1,0:T(4,128)(2,1)} %param.8) | data formatting | bytes 65536 | tf_op jit(solution)/shard_map/reshape | solution.py:371
  3.0 0.0 copy-start.2
  3.0 1.0 %copy.15 = bf16[8,8,16,128]{3,2,1,0:T(8,128)(2,1)S(1)} copy(bf16[8,8,16,128]{3,1,2,0:T(8,128)(2,1)} %bitcast.15) | data formatting | bytes 524288
  4.1 0.0 copy-start.3
  4.1 0.0 copy-done
  4.1 0.0 copy-done.2
  4.1 0.6 %copy-done.3 = f32[64]{0:T(128)S(1)} copy-done((f32[64]{0:T(128)S(1)}, f32[64]{0:T(128)}, u32[]{:S(2)}) %copy-start.3) | copy-done | bytes 280
  4.7 0.0 copy-start.1
  4.7 1.0 %copy-done.1 = bf16[27,64,64]{2,1,0:T(8,128)(2,1)S(1)} copy-done((bf16[27,64,64]{2,1,0:T(8,128)(2,1)S(1)}, bf16[27,64,64]{2,1,0:T(8,128)(2,1)}, u32[]{:S(2)}) %copy-start.1) | copy-done | bytes 221208
  5.7 41.5 %shard_map.119 = (bf16[8,8,16,128]{3,2,1,0:T(8,128)(2,1)S(1)}, bf16[4,4,16,64]{3,2,1,0:T(8,128)(2,1)S(1)}, f32[27,64,64]{2,1,0:T(8,128)S(1)}, f32[8,64,64]{2,1,0:T(8,128)S(1)}, f32[27,64,64]{2,1,0:T(8,128)S(1)}) custom-call(bf16[4,4,16,64]{3,2,1,0:T(8,128)(2,1)S(1)} %reshape.28.field, bf16[8,8,16,128]{3,2,1,0:T(8,128)(2,1)S(1)} %copy.15, ...), custom_call_target="tpu_custom_call" | custom-call | tf_op jit(solution)/shard_map/pallas_call | solution.py:381
  47.2 0.8 %reshape.32 = bf16[8,8,2048]{2,1,0:T(8,128)(2,1)} reshape(bf16[8,8,16,128]{3,2,1,0:T(8,128)(2,1)S(1)} %get-tuple-element.10) | data formatting | bytes 524288 | tf_op jit(solution)/shard_map/reshape | solution.py:408
  48.0 0.7 %reshape.33 = bf16[4,4,1024]{2,1,0:T(4,128)(2,1)} reshape(bf16[4,4,16,64]{3,2,1,0:T(8,128)(2,1)S(1)} %get-tuple-element.11) | data formatting | bytes 65536 | tf_op jit(solution)/shard_map/reshape | solution.py:408
  48.8 0.9 %copy.20 = f32[27,64,64]{2,1,0:T(8,128)} copy(f32[27,64,64]{2,1,0:T(8,128)S(1)} %get-tuple-element.22) | data formatting | bytes 884736
  49.7 0.7 %copy.21 = f32[8,64,64]{2,1,0:T(8,128)} copy(f32[8,64,64]{2,1,0:T(8,128)S(1)} %get-tuple-element.23) | data formatting | bytes 262144
  50.4 0.9 %copy.22 = f32[27,64,64]{2,1,0:T(8,128)} copy(f32[27,64,64]{2,1,0:T(8,128)S(1)} %get-tuple-element.24) | data formatting | bytes 884736
  (1 shorter events, 0.0 us)
Async XLA Ops:
  0.6 3.5 %copy-start = (bf16[27,64,64]{2,1,0:T(8,128)(2,1)S(1)}, bf16[27,64,64]{2,1,0:T(8,128)(2,1)}, u32[]{:S(2)}) copy-start(bf16[27,64,64]{2,1,0:T(8,128)(2,1)} %w_first.1) | copy-start | bytes 663556
  3.0 1.1 %copy-start.2 = (bf16[8,64,64]{2,1,0:T(8,128)(2,1)S(1)}, bf16[8,64,64]{2,1,0:T(8,128)(2,1)}, u32[]{:S(2)}) copy-start(bf16[8,64,64]{2,1,0:T(8,128)(2,1)} %w_upper.1) | copy-start | bytes 196612
  4.1 0.7 %copy-start.3 = (f32[64]{0:T(128)S(1)}, f32[64]{0:T(128)}, u32[]{:S(2)}) copy-start(f32[64]{0:T(128)} %param.10) | copy-start | bytes 772
  4.7 1.0 %copy-start.1 = (bf16[27,64,64]{2,1,0:T(8,128)(2,1)S(1)}, bf16[27,64,64]{2,1,0:T(8,128)(2,1)}, u32[]{:S(2)}) copy-start(bf16[27,64,64]{2,1,0:T(8,128)(2,1)} %w_second.1) | copy-start | bytes 663556

commit v4 on v3

--- a/solution.py
+++ b/solution.py
@@ -165,15 +165,12 @@
     return {1: pl.ds(0, width), -1: pl.ds(width + size, width), 0: pl.ds(width, size)}[step]
 
 
-def rim_copies(nx, ny, src, dst, width, send, recv, whole=False):
+def rim_copies(nx, ny, src, dst, width, send, recv):
     mx, my = lax.axis_index("gx"), lax.axis_index("gy")
     copies = []
     for k, (dx, dy) in enumerate(AROUND):
-        if whole:
-            part, spot = src, dst.at[1 - dx, 1 - dy]
-        else:
-            part = src.at[leaving(dx, src.shape[0], width), leaving(dy, src.shape[1], width)]
-            spot = dst.at[landing(dx, src.shape[0], width), landing(dy, src.shape[1], width)]
+        part = src.at[leaving(dx, src.shape[0], width), leaving(dy, src.shape[1], width)]
+        spot = dst.at[landing(dx, src.shape[0], width), landing(dy, src.shape[1], width)]
         copies.append(pltpu.make_async_remote_copy(
             src_ref=part, dst_ref=spot, send_sem=send.at[k], recv_sem=recv.at[k],
             device_id=(lax.rem(mx + dx + nx, nx), lax.rem(my + dy + ny, ny)), device_id_type=MESH))
@@ -227,14 +224,14 @@
     return jnp.concatenate([first, jnp.broadcast_to(mid, shape), last], axis=axis)
 
 
-def block_kernel(nx, ny, fine_scale, coarse_scale, field, cot, tile, w_first, b_first, w_upper, w_second, b_second,
+def block_kernel(nx, ny, fine_scale, coarse_scale, field, cot, w_first, b_first, w_upper, w_second, b_second,
                  out_field, out_grad, out_first, out_upper, out_second,
-                 field_ext, cot_ext, tile_ext, ctaps, ftaps, gtaps, rim_ext, rim_out,
-                 first_t, up_row, second_n, second_t, s_f, r_f, s_c, r_c, s_t, r_t, s_g, r_g, *groups):
+                 field_ext, cot_ext, ctaps, ftaps, gtaps, rim_ext, rim_out,
+                 first_t, up_row, second_n, second_t, s_f, r_f, s_c, r_c, s_g, r_g, *groups):
     mx, my = lax.axis_index("gx"), lax.axis_index("gy")
-    rows, cols, depth, chans = field.shape
+    rows, cols, depth, wide = field.shape
+    chans = wide // 2
     fr, fc = 2 * rows, 2 * cols
-    wide = 2 * chans
     part_a, full_a, *rest_a = groups[: len(groups) // 2]
     part_b, full_b, *rest_b = groups[len(groups) // 2 :]
     used_a, used_b = rest_a[0].shape[1], rest_b[0].shape[1]
@@ -246,12 +243,10 @@
     pl.semaphore_wait(barrier, len(peers))
     field_copies = rim_copies(nx, ny, field, field_ext, 2, s_f, r_f)
     cot_copies = rim_copies(nx, ny, cot, cot_ext, 1, s_c, r_c)
-    tile_copies = rim_copies(nx, ny, tile, tile_ext, 1, s_t, r_t, True)
-    for copy in field_copies + cot_copies + tile_copies:
+    for copy in field_copies + cot_copies:
         copy.start()
     field_ext[2 : 2 + rows, 2 : 2 + cols] = field[...]
     cot_ext[1 : 1 + fr, 1 : 1 + fc] = cot[...]
-    tile_ext[1, 1] = tile[...]
     none = jnp.zeros((chans, chans), jnp.bfloat16)
     for k in range(9):
         low, mid, high = w_second[3 * k], w_second[3 * k + 1], w_second[3 * k + 2]
@@ -266,7 +261,7 @@
     for copy in field_copies:
         copy.wait()
 
-    ctaps[...] = coarse_taps(field_ext[...])
+    ctaps[...] = coarse_taps(field_ext[..., :chans])
     pre_first = conv(ctaps, w_first[...].reshape(9, 3 * chans, chans), rows + 2, cols + 2) + b_first[...]
     small = jnp.exp(-jnp.abs(pre_first))
     hidden = act(pre_first, small).astype(jnp.bfloat16)
@@ -284,10 +279,13 @@
     pre_second = conv(ftaps, second_n, fr + 2, fc + 2) + b_second[...]
     small = jnp.exp(-jnp.abs(pre_second))
     out_field[...] = act(pre_second, small)[1 : 1 + fr, 1 : 1 + fc].astype(jnp.bfloat16)
-    for copy in cot_copies + tile_copies:
-        copy.wait()
-    tiles = tile_ext[...].astype(jnp.float32)
-    bands = [spread_edge([tiles[i, j][None] for j in range(3)], 0, fc)[None] for i in range(3)]
+    for copy in cot_copies:
+        copy.wait()
+    ends = ((0, 2, rows + 2), (0, 2, cols + 2))
+    bands = []
+    for i in ends[0]:
+        tiles = [field_ext[i, j, :, chans:].astype(jnp.float32) for j in ends[1]]
+        bands.append(spread_edge([jnp.concatenate([t, t], axis=1)[None] for t in tiles], 0, fc)[None])
     weight = spread_edge(bands, 0, fr)
     grad_pre = weight * cot_ext[...].astype(jnp.float32) * slope(pre_second, small)
     gtaps[..., :wide] = grad_pre.astype(jnp.bfloat16)
@@ -315,8 +313,8 @@
     corner = [six[:, a, :, b].reshape(-1, wide) for a in (0, 1) for b in (0, 1)]
     grad_hidden = times_t(jnp.concatenate(corner, axis=1), up_row[...])
     grad_first = (grad_hidden.reshape(rows, cols, depth, chans) * slope_first).astype(jnp.bfloat16)
-    rim_out[...] = grad_first
-    rim_ext[1 : 1 + rows, 1 : 1 + cols] = grad_first
+    rim_out[...] = jnp.concatenate([grad_first, jnp.zeros_like(grad_first)], axis=-1)
+    rim_ext[1 : 1 + rows, 1 : 1 + cols, :, :chans] = grad_first
     rim = rim_copies(nx, ny, rim_out, rim_ext, 1, s_g, r_g)
     for copy in rim:
         copy.start()
@@ -339,7 +337,7 @@
     next(sum_a)
     for copy in rim:
         copy.wait()
-    grad_in = conv(coarse_taps(rim_ext[...]), first_t, rows, cols, times_t)
+    grad_in = conv(coarse_taps(rim_ext[..., :chans]), first_t, rows, cols, times_t)
     out_grad[...] = grad_in.astype(jnp.bfloat16)
     next(sum_a)
     next(sum_b)
@@ -367,10 +365,10 @@
     fine_scale = 1.0 / math.sqrt(8 * rows * cols * depth * nx * ny)
     fr, fc = 2 * rows, 2 * cols
     bf, dma = jnp.bfloat16, pltpu.SemaphoreType.DMA
+    cells = field_in.reshape(rows, cols, depth, chans)
     args = (
-        field_in.reshape(rows, cols, depth, chans),
+        jnp.concatenate([cells, jnp.broadcast_to(tile_weights.astype(bf)[..., None, None], cells.shape)], axis=-1),
         cotangent.reshape(fr, fc, depth, wide),
-        jnp.broadcast_to(tile_weights.astype(bf), (16, wide)),
         w_first,
         b_first.reshape(1, chans),
         w_upper,
@@ -390,19 +388,18 @@
         in_specs=[vmem] * len(args),
         out_specs=(vmem,) * 5,
         scratch_shapes=[
-            pltpu.VMEM((rows + 4, cols + 4, depth, chans), bf),
+            pltpu.VMEM((rows + 4, cols + 4, depth, wide), bf),
             pltpu.VMEM((fr + 2, fc + 2, depth, wide), bf),
-            pltpu.VMEM((3, 3, 16, wide), bf),
             pltpu.VMEM((rows + 4, cols + 4, depth, 3 * chans), bf),
             pltpu.VMEM((fr + 4, fc + 4, depth, 2 * wide), bf),
             pltpu.VMEM((fr + 2, fc + 2, depth, 2 * wide), bf),
-            pltpu.VMEM((rows + 2, cols + 2, depth, chans), bf),
-            pltpu.VMEM((rows, cols, depth, chans), bf),
+            pltpu.VMEM((rows + 2, cols + 2, depth, wide), bf),
+            pltpu.VMEM((rows, cols, depth, wide), bf),
             pltpu.VMEM((9, chans, 3 * chans), bf),
             pltpu.VMEM((chans, 8 * chans), bf),
             pltpu.VMEM((9, 2 * wide, wide), bf),
             pltpu.VMEM((9, wide, 2 * wide), bf),
-        ] + [dma((8,))] * 8 + add_up_scratch(nx, ny, 14, chans) + add_up_scratch(nx, ny, 18, chans),
+        ] + [dma((8,))] * 6 + add_up_scratch(nx, ny, 14, chans) + add_up_scratch(nx, ny, 18, chans),
         compiler_params=pltpu.CompilerParams(collective_id=0, has_side_effects=True, vmem_limit_bytes=48 << 20),
     )(*args)
     return out.reshape(fr, fc, 2 * flat), grad.reshape(rows, cols, flat), first, upper, second

time: 51.6 us -> 51.3 us (level)
  no operation moved by 1% of the time
where the time goes in v4:
time: 51.3 us; the launch traced here: 51 us
  Pallas kernels  41.2 us (80%)
  local copies, waits for them, and re-layouts  7.63 us (15%)
  between operations  1.41 us (3%)
  other arithmetic  0.81 us (2%)
    pallas_call x1, Pallas kernels, per_device(): pl.pallas_call(functools.partial(block_kernel, nx, ny, fine_scale, coarse...  41.2 us
    unnamed x12, local copies, waits for them, and re-layouts  5.2 us

profile of v4, /device:TPU:0, one launch (start us, length us, event | category | flops | bytes accessed | tf_op | source)
XLA Modules:
  0.0 51.0 jit_solution(8861543314168408902)
XLA Ops:
  0.6 0.0 copy-start
  1.3 0.8 %maximum_bitcast_fusion.b_second = f32[1,128]{1,0:T(1,128)S(1)} fusion(f32[64]{0:T(128)} %param.13), kind=kLoop, calls=%fused_computation.1 | loop fusion | flops 128 | bytes 768 | tf_op jit(solution)/shard_map/reshape | solution.py:376
  2.2 0.9 %reshape.29 = bf16[4,4,16,64]{3,2,1,0:T(8,128)(2,1)S(1)} reshape(bf16[4,4,1024]{2,1,0:T(4,128)(2,1)} %param.8) | data formatting | bytes 65536 | tf_op jit(solution)/shard_map/reshape | solution.py:368
  3.0 0.0 copy-start.2
  3.1 1.0 %copy.15 = bf16[8,8,16,128]{3,2,1,0:T(8,128)(2,1)S(1)} copy(bf16[8,8,16,128]{3,1,2,0:T(8,128)(2,1)} %bitcast.15) | data formatting | bytes 524288
  4.1 0.0 copy-start.3
  4.1 0.0 copy-done
  4.1 0.0 copy-done.2
  4.1 0.6 %copy-done.3 = f32[64]{0:T(128)S(1)} copy-done((f32[64]{0:T(128)S(1)}, f32[64]{0:T(128)}, u32[]{:S(2)}) %copy-start.3) | copy-done | bytes 280
  4.8 0.0 copy-start.1
  4.8 1.0 %copy-done.1 = bf16[27,64,64]{2,1,0:T(8,128)(2,1)S(1)} copy-done((bf16[27,64,64]{2,1,0:T(8,128)(2,1)S(1)}, bf16[27,64,64]{2,1,0:T(8,128)(2,1)}, u32[]{:S(2)}) %copy-start.1) | copy-done | bytes 221208
  5.8 41.2 %shard_map.119 = (bf16[8,8,16,128]{3,2,1,0:T(8,128)(2,1)S(1)}, bf16[4,4,16,64]{3,2,1,0:T(8,128)(2,1)S(1)}, f32[27,64,64]{2,1,0:T(8,128)S(1)}, f32[8,64,64]{2,1,0:T(8,128)S(1)}, f32[27,64,64]{2,1,0:T(8,128)S(1)}) custom-call(bf16[4,4,16,128]{3,2,1,0:T(8,128)(2,1)S(1)} %concatenate.6.field, bf16[8,8,16,128]{3,2,1,0:T(8,128)(2,1)S(1)} %copy.15, ...), custom_call_target="tpu_custom_call" | custom-call | tf_op jit(solution)/shard_map/pallas_call | solution.py:379
  46.9 0.8 %reshape.33 = bf16[8,8,2048]{2,1,0:T(8,128)(2,1)} reshape(bf16[8,8,16,128]{3,2,1,0:T(8,128)(2,1)S(1)} %get-tuple-element.10) | data formatting | bytes 524288 | tf_op jit(solution)/shard_map/reshape | solution.py:405
  47.8 0.7 %reshape.34 = bf16[4,4,1024]{2,1,0:T(4,128)(2,1)} reshape(bf16[4,4,16,64]{3,2,1,0:T(8,128)(2,1)S(1)} %get-tuple-element.11) | data formatting | bytes 65536 | tf_op jit(solution)/shard_map/reshape | solution.py:405
  48.5 0.9 %copy.20 = f32[27,64,64]{2,1,0:T(8,128)} copy(f32[27,64,64]{2,1,0:T(8,128)S(1)} %get-tuple-element.22) | data formatting | bytes 884736
  49.4 0.7 %copy.21 = f32[8,64,64]{2,1,0:T(8,128)} copy(f32[8,64,64]{2,1,0:T(8,128)S(1)} %get-tuple-element.23) | data formatting | bytes 262144
  50.1 0.9 %copy.22 = f32[27,64,64]{2,1,0:T(8,128)} copy(f32[27,64,64]{2,1,0:T(8,128)S(1)} %get-tuple-element.24) | data formatting | bytes 884736
  (1 shorter events, 0.0 us)
Async XLA Ops:
  0.6 3.5 %copy-start = (bf16[27,64,64]{2,1,0:T(8,128)(2,1)S(1)}, bf16[27,64,64]{2,1,0:T(8,128)(2,1)}, u32[]{:S(2)}) copy-start(bf16[27,64,64]{2,1,0:T(8,128)(2,1)} %w_first.1) | copy-start | bytes 663556
  3.0 1.1 %copy-start.2 = (bf16[8,64,64]{2,1,0:T(8,128)(2,1)S(1)}, bf16[8,64,64]{2,1,0:T(8,128)(2,1)}, u32[]{:S(2)}) copy-start(bf16[8,64,64]{2,1,0:T(8,128)(2,1)} %w_upper.1) | copy-start | bytes 196612
  4.1 0.7 %copy-start.3 = (f32[64]{0:T(128)S(1)}, f32[64]{0:T(128)}, u32[]{:S(2)}) copy-start(f32[64]{0:T(128)} %param.10) | copy-start | bytes 772
  4.8 1.0 %copy-start.1 = (bf16[27,64,64]{2,1,0:T(8,128)(2,1)S(1)}, bf16[27,64,64]{2,1,0:T(8,128)(2,1)}, u32[]{:S(2)}) copy-start(bf16[27,64,64]{2,1,0:T(8,128)(2,1)} %w_second.1) | copy-start | bytes 663556

commit v5 on v4

--- a/solution.py
+++ b/solution.py
@@ -276,7 +276,7 @@
     ftaps[..., :wide] = upper.astype(jnp.bfloat16)
     ftaps[..., wide:] = fine_taps(ftaps[..., :wide].astype(jnp.float32))
 
-    pre_second = conv(ftaps, second_n, fr + 2, fc + 2) + b_second[...]
+    pre_second = conv(ftaps, second_n, fr + 2, fc + 2) + jnp.concatenate([b_second[...], b_second[...]], axis=1)
     small = jnp.exp(-jnp.abs(pre_second))
     out_field[...] = act(pre_second, small)[1 : 1 + fr, 1 : 1 + fc].astype(jnp.bfloat16)
     for copy in cot_copies:
@@ -373,7 +373,7 @@
         b_first.reshape(1, chans),
         w_upper,
         w_second,
-        jnp.concatenate([b_second, b_second]).reshape(1, wide),
+        b_second.reshape(1, chans),
     )
     vmem = pl.BlockSpec(memory_space=pltpu.VMEM)
     out, grad, first, upper, second = pl.pallas_call(

time: 51.3 us -> 50.5 us (0.984)
  other arithmetic: 0.81 us -> 0 us
    reshape x1 -> x0, other arithmetic: 0.81 us -> none  [per_device(): jnp.concatenate([b_second, b_second]).reshape(1, wide)]
    unnamed x12 -> x14, local copies, waits for them, and re-layouts: 5.2 us -> 5.21 us
where the time goes in v5:
time: 50.5 us; the launch traced here: 50.2 us
  Pallas kernels  41.2 us (82%)
  local copies, waits for them, and re-layouts  7.64 us (15%)
  between operations  1.42 us (3%)
    pallas_call x1, Pallas kernels, per_device(): pl.pallas_call(functools.partial(block_kernel, nx, ny, fine_scale, coarse...  41.2 us
    unnamed x14, local copies, waits for them, and re-layouts  5.21 us

profile of v5, /device:TPU:0, one launch (start us, length us, event | category | flops | bytes accessed | tf_op | source)
XLA Modules:
  0.0 50.2 jit_solution(10167942575319349256)
XLA Ops:
  0.6 0.0 copy-start
  1.3 0.9 %reshape.29 = bf16[4,4,16,64]{3,2,1,0:T(8,128)(2,1)S(1)} reshape(bf16[4,4,1024]{2,1,0:T(4,128)(2,1)} %param.8) | data formatting | bytes 65536 | tf_op jit(solution)/shard_map/reshape | solution.py:368
  2.2 0.0 copy-start.2
  2.3 1.0 %copy.15 = bf16[8,8,16,128]{3,2,1,0:T(8,128)(2,1)S(1)} copy(bf16[8,8,16,128]{3,1,2,0:T(8,128)(2,1)} %bitcast.15) | data formatting | bytes 524288
  3.3 0.0 copy-start.3
  3.3 0.0 copy-start.4
  3.3 0.0 copy-done
  3.3 0.0 copy-done.2
  3.3 0.6 %copy-done.3 = f32[64]{0:T(128)S(1)} copy-done((f32[64]{0:T(128)S(1)}, f32[64]{0:T(128)}, u32[]{:S(2)}) %copy-start.3) | copy-done | bytes 280
  3.9 0.0 copy-done.4
  4.0 0.0 copy-start.1
  4.0 1.0 %copy-done.1 = bf16[27,64,64]{2,1,0:T(8,128)(2,1)S(1)} copy-done((bf16[27,64,64]{2,1,0:T(8,128)(2,1)S(1)}, bf16[27,64,64]{2,1,0:T(8,128)(2,1)}, u32[]{:S(2)}) %copy-start.1) | copy-done | bytes 221208
  5.0 41.2 %shard_map.119 = (bf16[8,8,16,128]{3,2,1,0:T(8,128)(2,1)S(1)}, bf16[4,4,16,64]{3,2,1,0:T(8,128)(2,1)S(1)}, f32[27,64,64]{2,1,0:T(8,128)S(1)}, f32[8,64,64]{2,1,0:T(8,128)S(1)}, f32[27,64,64]{2,1,0:T(8,128)S(1)}) custom-call(bf16[4,4,16,128]{3,2,1,0:T(8,128)(2,1)S(1)} %concatenate.3.field, bf16[8,8,16,128]{3,2,1,0:T(8,128)(2,1)S(1)} %copy.15, ...), custom_call_target="tpu_custom_call" | custom-call | tf_op jit(solution)/shard_map/pallas_call | solution.py:379
  46.1 0.8 %reshape.33 = bf16[8,8,2048]{2,1,0:T(8,128)(2,1)} reshape(bf16[8,8,16,128]{3,2,1,0:T(8,128)(2,1)S(1)} %get-tuple-element.10) | data formatting | bytes 524288 | tf_op jit(solution)/shard_map/reshape | solution.py:405
  47.0 0.7 %reshape.34 = bf16[4,4,1024]{2,1,0:T(4,128)(2,1)} reshape(bf16[4,4,16,64]{3,2,1,0:T(8,128)(2,1)S(1)} %get-tuple-element.11) | data formatting | bytes 65536 | tf_op jit(solution)/shard_map/reshape | solution.py:405
  47.7 0.9 %copy.20 = f32[27,64,64]{2,1,0:T(8,128)} copy(f32[27,64,64]{2,1,0:T(8,128)S(1)} %get-tuple-element.22) | data formatting | bytes 884736
  48.6 0.7 %copy.21 = f32[8,64,64]{2,1,0:T(8,128)} copy(f32[8,64,64]{2,1,0:T(8,128)S(1)} %get-tuple-element.23) | data formatting | bytes 262144
  49.3 0.9 %copy.22 = f32[27,64,64]{2,1,0:T(8,128)} copy(f32[27,64,64]{2,1,0:T(8,128)S(1)} %get-tuple-element.24) | data formatting | bytes 884736
  (1 shorter events, 0.0 us)
Async XLA Ops:
  0.6 2.7 %copy-start = (bf16[27,64,64]{2,1,0:T(8,128)(2,1)S(1)}, bf16[27,64,64]{2,1,0:T(8,128)(2,1)}, u32[]{:S(2)}) copy-start(bf16[27,64,64]{2,1,0:T(8,128)(2,1)} %w_first.1) | copy-start | bytes 663556
  2.2 1.1 %copy-start.2 = (bf16[8,64,64]{2,1,0:T(8,128)(2,1)S(1)}, bf16[8,64,64]{2,1,0:T(8,128)(2,1)}, u32[]{:S(2)}) copy-start(bf16[8,64,64]{2,1,0:T(8,128)(2,1)} %w_upper.1) | copy-start | bytes 196612
  3.3 0.7 %copy-start.3 = (f32[64]{0:T(128)S(1)}, f32[64]{0:T(128)}, u32[]{:S(2)}) copy-start(f32[64]{0:T(128)} %param.10) | copy-start | bytes 772
  3.3 0.7 %copy-start.4 = (f32[64]{0:T(128)S(1)}, f32[64]{0:T(128)}, u32[]{:S(2)}) copy-start(f32[64]{0:T(128)} %param.13) | copy-start | bytes 772
  4.0 1.0 %copy-start.1 = (bf16[27,64,64]{2,1,0:T(8,128)(2,1)S(1)}, bf16[27,64,64]{2,1,0:T(8,128)(2,1)}, u32[]{:S(2)}) copy-start(bf16[27,64,64]{2,1,0:T(8,128)(2,1)} %w_second.1) | copy-start | bytes 663556
